TPU v7x, 512 devices: a whole 4x8x8 slice. The times are simulated.
512 devices in a mesh: lon: 32 (over z_hi, y, core), lat: 16 (over z_lo, x).
Axes of the slice: x: 4, y: 8, z: 8 (z_hi: 2, z_lo: 4; z = z_hi * 4 + z_lo), core: 2. Of those that a mesh axis runs over, the one named last changes fastest.
Arguments:
- ocean_state: float32 [3, 8, 256, 4096], P(None, None, 'lat', 'lon'), may hold values from -6 to 6
- diffusivity: float32 [8, 256, 4096], P(None, 'lat', 'lon'), may hold values from 0.02 to 0.22
- depth_levels: int32 [256, 4096], P('lat', 'lon'), may hold values from 0 to 8, as said below
- fold_pair: int32 [4096], replicated, may hold values from 0 to 4095, as said below
- first_weight: bfloat16 [9, 64, 24], replicated, may hold values from -0.4375 to 0.4375
- mix_weight: bfloat16 [64, 64], replicated, may hold values from -0.75 to 0.75
- last_weight: bfloat16 [9, 16, 64], replicated, may hold values from -0.25 to 0.25
- cotangent: bfloat16 [16, 256, 4096], P(None, 'lat', 'lon'), may hold values from -6 to 6
- active_index: int32 [8192], replicated, may hold values from 0 to 27135, as said below
Outputs:
- new_state: float32 [3, 8, 256, 4096], P(None, None, 'lat', 'lon')
- closure: bfloat16 [16, 256, 4096], P(None, 'lat', 'lon')
- grad_active: float32 [8192], replicated
Inputs may be any that keep to these rules, and one draw needn't show every extreme that they name: `depth_levels`: 0 marks land; otherwise the number of wet levels of the column. fold_pair[i] = (s - i) mod 4096 for one s, the same for every i. `active_index`: distinct entries; 0 and 27135 are always among them.
All inputs are finite; a program needn't handle non-finite values.
Results may differ from a plain program's by a relative error of at most 0.0065.
Values may be sent and summed in bfloat16 or wider, within the bound.
No kernel may reach another device: no remote copies, remote signals or barrier semaphores. Data moves between devices by JAX's collectives and lax.ppermute only.
A program may use at most 64 MiB of HBM per device.

v0:
```python
import math

import jax
import jax.numpy as jnp
from jax import lax
from jax.sharding import PartitionSpec as P

coriolis_peak = 0.25
pressure_scale = 0.05
advect_scale = 0.25


def padded_2(cells, sides, width):
    for axis, dim in sides:
        count = lax.axis_size(axis)
        head = lax.slice_in_dim(cells, 0, width, axis=dim)
        tail = lax.slice_in_dim(cells, cells.shape[dim] - width, cells.shape[dim], axis=dim)
        cells = jnp.concatenate(
            [
                lax.ppermute(tail, axis, [(i, (i + 1) % count) for i in range(count)]),
                cells,
                lax.ppermute(head, axis, [((i + 1) % count, i) for i in range(count)]),
            ],
            axis=dim,
        )
    return cells


def coriolis(row_ids, row_total):
    mirrored = jnp.where(row_ids >= row_total, 2 * row_total - 1 - row_ids, row_ids)
    return coriolis_peak * jnp.sin(
        math.pi * (mirrored.astype(jnp.float32) + 0.5) / row_total - 0.5 * math.pi
    )


def offset_view(field, shift_row, shift_col):
    height = field.shape[1] - 2
    width = field.shape[2] - 2
    return field[:, 1 + shift_row : 1 + shift_row + height, 1 + shift_col : 1 + shift_col + width]


def stencil(padded, coriolis_rows):
    u_all = padded[0]
    v_all = padded[1]
    t_all = padded[2]
    k_all = padded[3]
    k_center = offset_view(k_all, 0, 0)
    k_east = jnp.sqrt(k_center * offset_view(k_all, 0, 1))
    k_west = jnp.sqrt(k_center * offset_view(k_all, 0, -1))
    k_north = jnp.sqrt(k_center * offset_view(k_all, 1, 0))
    k_south = jnp.sqrt(k_center * offset_view(k_all, -1, 0))

    def diffuse(field):
        middle = offset_view(field, 0, 0)
        return (
            k_east * (offset_view(field, 0, 1) - middle)
            + k_west * (offset_view(field, 0, -1) - middle)
            + k_north * (offset_view(field, 1, 0) - middle)
            + k_south * (offset_view(field, -1, 0) - middle)
        )

    pressure = pressure_scale * jnp.cumsum(t_all, axis=0)
    wet_here = (k_center > 0).astype(jnp.float32)
    f_rows = coriolis_rows[None, :, None]
    u_mid = offset_view(u_all, 0, 0)
    v_mid = offset_view(v_all, 0, 0)
    t_mid = offset_view(t_all, 0, 0)
    u_change = f_rows * v_mid - 0.5 * (offset_view(pressure, 0, 1) - offset_view(pressure, 0, -1))
    v_change = -f_rows * u_mid - 0.5 * (offset_view(pressure, 1, 0) - offset_view(pressure, -1, 0))
    t_change = (
        -advect_scale
        * 0.5
        * (
            u_mid * (offset_view(t_all, 0, 1) - offset_view(t_all, 0, -1))
            + v_mid * (offset_view(t_all, 1, 0) - offset_view(t_all, -1, 0))
        )
    )
    return jnp.stack(
        [
            wet_here * (u_mid + u_change + diffuse(u_all)),
            wet_here * (v_mid + v_change + diffuse(v_all)),
            wet_here * (t_mid + t_change + diffuse(t_all)),
        ]
    )


def convolve(padded, weight):
    height = padded.shape[1] - 2
    width = padded.shape[2] - 2
    summed = None
    for tap_index in range(9):
        tap_row = tap_index // 3
        tap_col = tap_index % 3
        term = jnp.einsum(
            "oc,cyx->oyx",
            weight[tap_index],
            padded[:, tap_row : tap_row + height, tap_col : tap_col + width],
            preferred_element_type=jnp.float32,
        )
        summed = term if tap_index == 0 else summed + term
    return summed


def convolve_back(padded, weight):
    height = padded.shape[1] - 2
    width = padded.shape[2] - 2
    summed = None
    for tap_index in range(9):
        tap_row = tap_index // 3
        tap_col = tap_index % 3
        term = jnp.einsum(
            "oc,oyx->cyx",
            weight[tap_index],
            padded[:, 2 - tap_row : 2 - tap_row + height, 2 - tap_col : 2 - tap_col + width],
            preferred_element_type=jnp.float32,
        )
        summed = term if tap_index == 0 else summed + term
    return summed


def tap_grads(grad, padded):
    height = grad.shape[1]
    width = grad.shape[2]
    terms = []
    for tap_index in range(9):
        tap_row = tap_index // 3
        tap_col = tap_index % 3
        terms.append(
            jnp.einsum(
                "oyx,cyx->oc",
                grad,
                padded[:, tap_row : tap_row + height, tap_col : tap_col + width],
                preferred_element_type=jnp.float32,
            )
        )
    return jnp.stack(terms)


def silu_slope(pre):
    sigma = jax.nn.sigmoid(pre)
    return sigma * (1.0 + pre * (1.0 - sigma))


def on_device(
    ocean_state,
    diffusivity,
    depth_levels,
    fold_pair,
    first_weight,
    mix_weight,
    last_weight,
    cotangent,
    active_index,
):
    depth_count = ocean_state.shape[1]
    row_count = ocean_state.shape[2]
    col_count = ocean_state.shape[3]
    lat_index = lax.axis_index("lat")
    lon_index = lax.axis_index("lon")
    row_total = row_count * lax.axis_size("lat")
    col_total = col_count * lax.axis_size("lon")
    at_top = lat_index == lax.axis_size("lat") - 1
    at_bottom = lat_index == 0
    first_row = lat_index * row_count
    level_ids = jnp.arange(depth_count, dtype=jnp.int32)
    wet_mask = (level_ids[:, None, None] < depth_levels[None]).astype(jnp.float32)
    wet_kappa = diffusivity * wet_mask
    fields = ocean_state * wet_mask[None]
    fold_signs = jnp.concatenate(
        [-jnp.ones((2 * depth_count,), jnp.float32), jnp.ones((2 * depth_count,), jnp.float32)]
    )
    own_rows = first_row + jnp.arange(row_count, dtype=jnp.int32)
    for step_index in range(2):
        source = jnp.concatenate([fields, wet_kappa[None]], axis=0).reshape(
            4 * depth_count, row_count, col_count
        )
        rim = padded_2(source, (("lon", 2), ("lat", 1)), 1)
        top_rows = lax.all_gather(source[:, row_count - 1 :, :], "lon", axis=2, tiled=True)
        col_ids = (
            lon_index * col_count - 1 + jnp.arange(col_count + 2 * 1, dtype=jnp.int32)
        ) % col_total
        partner = jnp.take(fold_pair, col_ids)
        north_rows = jnp.stack(
            [fold_signs[:, None] * jnp.take(top_rows[:, 1 - 1, :], partner, axis=1)], axis=1
        )
        close_height = rim.shape[1]
        close_upper = jnp.where(at_top, north_rows, rim[:, close_height - 1 :, :])
        close_lower = jnp.where(at_bottom, jnp.zeros_like(north_rows), rim[:, :1, :])
        padded = jnp.concatenate(
            [close_lower, rim[:, 1 : close_height - 1, :], close_upper], axis=1
        ).reshape(4, depth_count, row_count + 2, col_count + 2)
        fields = stencil(padded, coriolis(own_rows, row_total))

    def open_deep(rim, margin):
        height = rim.shape[1]
        upper = jnp.where(
            at_top, jnp.zeros_like(rim[:, height - margin :, :]), rim[:, height - margin :, :]
        )
        lower = jnp.where(at_bottom, jnp.zeros_like(rim[:, :margin, :]), rim[:, :margin, :])
        return jnp.concatenate([lower, rim[:, margin : height - margin, :], upper], axis=1)

    in_channels = 3 * depth_count
    inputs = fields.reshape(in_channels, row_count, col_count).astype(jnp.bfloat16)
    level_mask = jnp.concatenate([wet_mask, wet_mask], axis=0)
    grad_scale = 1.0 / math.sqrt(row_total * col_total)
    out_grad = (grad_scale * level_mask * cotangent.astype(jnp.float32)).astype(jnp.bfloat16)
    stacked_net = jnp.concatenate([inputs, out_grad], axis=0)
    joined = open_deep(padded_2(stacked_net, (("lon", 2), ("lat", 1)), 1), 1)
    x_rim = joined[:in_channels]
    g_rim = joined[in_channels:]
    pre_first = convolve(x_rim, first_weight)
    hidden_first = jax.nn.silu(pre_first).astype(jnp.bfloat16)
    pre_mix = jnp.einsum(
        "oc,cyx->oyx", mix_weight, hidden_first, preferred_element_type=jnp.float32
    )
    hidden_mix = jax.nn.silu(pre_mix).astype(jnp.bfloat16)
    h_rim = open_deep(padded_2(hidden_mix, (("lon", 2), ("lat", 1)), 1), 1)
    closure = (level_mask * convolve(h_rim, last_weight)).astype(jnp.bfloat16)
    grad_last = tap_grads(out_grad, h_rim)
    back_mix = convolve_back(g_rim, last_weight)
    delta_mix = (back_mix * silu_slope(pre_mix)).astype(jnp.bfloat16)
    grad_mix = jnp.einsum(
        "oyx,cyx->oc", delta_mix, hidden_first, preferred_element_type=jnp.float32
    )
    back_first = jnp.einsum(
        "oc,oyx->cyx", mix_weight, delta_mix, preferred_element_type=jnp.float32
    )
    delta_first = (back_first * silu_slope(pre_first)).astype(jnp.bfloat16)
    grad_first = tap_grads(delta_first, x_rim)
    flat = jnp.concatenate([grad_first.reshape(-1), grad_mix.reshape(-1), grad_last.reshape(-1)])
    grad_active = jnp.take(lax.psum(flat, ("lon", "lat")), active_index)
    return (fields, closure, grad_active)


def solution(mesh):
    in_specs = (
        P(None, None, "lat", "lon"),
        P(None, "lat", "lon"),
        P("lat", "lon"),
        P(),
        P(),
        P(),
        P(),
        P(None, "lat", "lon"),
        P(),
    )
    out_specs = (P(None, None, "lat", "lon"), P(None, "lat", "lon"), P())
    return jax.shard_map(
        on_device, mesh=mesh, in_specs=in_specs, out_specs=out_specs, check_vma=False
    )
```

profile of v0, /device:TPU:1, one launch (start us, length us, event | category | flops | bytes accessed | tf_op | source)
XLA Modules:
  0.0 562.0 jit_solution(16202863687473160955)
XLA Ops:
  7.2 0.7 fusion.150
  7.9 0.9 fusion.227
  8.8 1.0 copy_multiply_fusion
  10.0 4.7 collective-permute-start
  14.8 6.1 %collective-permute-start.1 = (f32[32,16,1]{2,0,1:T(8,128)S(1)}, f32[32,16,1]{2,0,1:T(8,128)S(1)}, u32[]{:S(2)}, u32[]{:S(2)}) collective-permute-start(f32[32,16,1]{2,0,1:T(8,128)S(1)} %get-tuple-element.32), channel_id=1, source_target_pairs={{16,0},{32,16},{48,32},{64,48},{80,64},{96,80},{112,96},{128,112},... | collective-permute-start | bytes 6152 | tf_op jit(solution)/shard_map/ppermute | solution.py:22
  20.9 61.6 %all_gather.6 = f32[32,1,4096]{2,0,1:T(8,128)} all-gather(f32[32,1,128]{2,0,1:T(8,128)S(1)} %slice.669), channel_id=1, replica_groups=mesh['lon'=32,'lat'=16] {'lon'}, dimensions={2}, use_global_device_ids=true | all-gather | bytes 540672 | tf_op jit(solution)/shard_map/all_gather | solution.py:178
  82.5 1.4 gather_fusion.1
  84.0 0.6 fusion.151
  84.6 1.1 fusion.181
  85.7 0.7 pad_maximum_fusion.53
  86.4 2.9 collective-permute-start.2
  89.4 1.6 copy.26
  91.0 0.7 gather_fusion.2
  91.8 6.3 %collective-permute-start.3 = (f32[32,1,130]{2,0,1:T(8,128)}, f32[32,1,130]{2,0,1:T(8,128)S(1)}, u32[]{:S(2)}, u32[]{:S(2)}) collective-permute-start(f32[32,1,130]{2,0,1:T(8,128)} %get-tuple-element.19), channel_id=1, source_target_pairs={{1,0},{2,1},{3,2},{4,3},{5,4},{6,5},{7,6},{8,7},{9,8},{10,9},{11,1... | collective-permute-start | bytes 49928 | tf_op jit(solution)/shard_map/ppermute | solution.py:22
  98.1 1.3 collective-permute-done.3
  100.7 0.8 constant_dynamic-update-slice_fusion.1
  101.6 0.9 fusion.230
  102.5 1.9 collective-permute-start.4
  104.4 3.2 collective-permute-start.5
  107.6 66.3 %all_gather.7 = f32[32,1,4096]{0,2,1:T(8,128)S(1)} all-gather(f32[32,1,128]{0,2,1:T(8,128)S(1)} %copy.47), channel_id=1, replica_groups=mesh['lon'=32,'lat'=16] {'lon'}, dimensions={2}, use_global_device_ids=true | all-gather | bytes 540672 | tf_op jit(solution)/shard_map/all_gather | solution.py:178
  174.0 0.7 gather_fusion.3
  174.8 8.6 %collective-permute-start.7 = (f32[32,1,130]{2,0,1:T(8,128)S(1)}, f32[32,1,130]{2,0,1:T(8,128)S(1)}, u32[]{:S(2)}, u32[]{:S(2)}) collective-permute-start(f32[32,1,130]{2,0,1:T(8,128)S(1)} %get-tuple-element.17), channel_id=1, source_target_pairs={{1,0},{2,1},{3,2},{4,3},{5,4},{6,5},{7,6},{8,7},{9,8},{10,9},{11,1... | collective-permute-start | bytes 49928 | tf_op jit(solution)/shard_map/ppermute | solution.py:22
  183.4 1.9 collective-permute-start.6
  185.4 0.7 constant_dynamic-update-slice_fusion
  186.1 5.9 %collective-permute-done.6 = f32[32,1,130]{2,0,1:T(8,128)S(1)} collective-permute-done((f32[32,1,130]{2,0,1:T(8,128)S(1)}, f32[32,1,130]{2,0,1:T(8,128)S(1)}, u32[]{:S(2)}, u32[]{:S(2)}) %collective-permute-start.6) | collective-permute-done | bytes 16672 | tf_op jit(solution)/shard_map/ppermute | solution.py:20
  193.3 1.9 collective-permute-start.8
  195.3 3.5 collective-permute-start.9
  199.1 0.7 copy.43
  199.8 2.1 collective-permute-done.9
  202.0 2.0 collective-permute-start.11
  204.0 3.3 collective-permute-start.10
  207.5 5.0 collective-permute-done.10
  215.4 0.4 multiply_convert_fusion.1
  216.9 0.5 copy-done.3
  218.3 0.4 fusion.9
  218.7 0.3 fusion.8
  220.7 3.2 collective-permute-start.12
  223.9 9.2 %collective-permute-start.13 = (bf16[64,16,1]{2,0,1:T(8,128)(2,1)S(1)}, bf16[64,16,1]{2,0,1:T(8,128)(2,1)S(1)}, u32[]{:S(2)}, u32[]{:S(2)}) collective-permute-start(bf16[64,16,1]{2,0,1:T(8,128)(2,1)S(1)} %get-tuple-element.26), channel_id=1, source_target_pairs={{16,0},{32,16},{48,32},{64,48},{80,64},{96,80},{112,96},{128,112},... | collective-permute-start | bytes 6152 | tf_op jit(solution)/shard_map/ppermute | solution.py:22
  233.4 0.9 collective-permute-done.13
  234.3 1.9 collective-permute-start.15
  236.9 3.5 collective-permute-start.14
  240.5 5.0 collective-permute-done.14
  245.5 0.5 maximum_maximum_fusion
  248.7 0.7 pad_maximum_fusion.17
  250.9 0.7 copy.44
  251.5 265.4 %all-reduce.2.cloned.1.call-done = f32[27136]{0:T(1024)} async-done(((f32[27136]{0:T(1024)}), f32[27136]{0:T(1024)}) %all-reduce.2.cloned.1.call-update) | async-done | bytes 108560 | tf_op jit(solution)/shard_map/psum | solution.py:231
  517.0 37.5 %gather_fusion = f32[8192]{0:T(1024)S(1)} fusion(f32[27136]{0:T(1024)} %all-reduce.2.cloned.1.call-done, s32[8192]{0:T(1024)S(1)} %copy-done.9), kind=kCustom, calls=%fused_computation.3 | custom fusion | bytes 98304 | tf_op jit(solution)/shard_map/jit(_take)/gather | solution.py:231
  554.5 0.6 and_select_fusion
  (131 shorter events, 15.6 us)
Async XLA Ops:
  7.2 208.6 %copy-start = (bf16[64,64]{1,0:T(8,128)(2,1)S(1)}, bf16[64,64]{1,0:T(8,128)(2,1)}, u32[]{:S(2)}) copy-start(bf16[64,64]{1,0:T(8,128)(2,1)} %param.18) | copy-start | bytes 24580
  7.2 509.8 %all-reduce.2.cloned.1.call-start = ((), (), s32[]{:S(2)}) async-start(), calls=%async_computation | async-start | bytes 221184 | tf_op jit(solution)/shard_map/psum | solution.py:231
  9.8 72.7 %copy-start.1 = (s32[4096]{0:T(1024)S(1)}, s32[4096]{0:T(1024)}, u32[]{:S(2)}) copy-start(s32[4096]{0:T(1024)} %param.16) | copy-start | bytes 49156
  9.8 74.1 %copy-start.10 = (bf16[16,16,128]{2,1,0:T(8,128)(2,1)S(1)}, bf16[16,16,128]{2,1,0:T(8,128)(2,1)}, u32[]{:S(2)}) copy-start(bf16[16,16,128]{2,1,0:T(8,128)(2,1)} %param.20) | copy-start | bytes 196612
  10.0 74.0 %copy-start.7 = (s32[8192]{0:T(1024)S(1)}, s32[8192]{0:T(1024)}, u32[]{:S(2)}) copy-start(s32[8192]{0:T(1024)} %param.21) | copy-start | bytes 98308
  10.0 74.6 %copy-start.6 = (bf16[9,16,64]{2,1,0:T(8,128)(2,1)S(1)}, bf16[9,16,64]{2,1,0:T(8,128)(2,1)}, u32[]{:S(2)}) copy-start(bf16[9,16,64]{2,1,0:T(8,128)(2,1)} %param.19) | copy-start | bytes 55300
  10.0 75.7 %collective-permute-start = (f32[32,16,1]{2,0,1:T(8,128)S(1)}, f32[32,16,1]{2,0,1:T(8,128)S(1)}, u32[]{:S(2)}, u32[]{:S(2)}) collective-permute-start(f32[32,16,1]{2,0,1:T(8,128)S(1)} %get-tuple-element.31), channel_id=1, source_target_pairs={{0,16},{16,32},{32,48},{48,64},{64,80},{80,96},{96,112},{112,128},... | collective-permute-start | bytes 6152 | tf_op jit(solution)/shard_map/ppermute | solution.py:20
  14.8 70.9 %collective-permute-start.1 = (f32[32,16,1]{2,0,1:T(8,128)S(1)}, f32[32,16,1]{2,0,1:T(8,128)S(1)}, u32[]{:S(2)}, u32[]{:S(2)}) collective-permute-start(f32[32,16,1]{2,0,1:T(8,128)S(1)} %get-tuple-element.32), channel_id=1, source_target_pairs={{16,0},{32,16},{48,32},{64,48},{80,64},{96,80},{112,96},{128,112},... | collective-permute-start | bytes 6152 | tf_op jit(solution)/shard_map/ppermute | solution.py:22
  86.4 11.7 %collective-permute-start.2 = (f32[32,1,130]{2,0,1:T(8,128)}, f32[32,1,130]{2,0,1:T(8,128)}, u32[]{:S(2)}, u32[]{:S(2)}) collective-permute-start(f32[32,1,130]{2,0,1:T(8,128)} %get-tuple-element.20), channel_id=1, source_target_pairs={{0,1},{1,2},{2,3},{3,4},{4,5},{5,6},{6,7},{7,8},{8,9},{9,10},{10,1... | collective-permute-start | bytes 49928 | tf_op jit(solution)/shard_map/ppermute | solution.py:20
  89.3 10.1 %copy-start.12 = (f32[32]{0:T(128)S(1)}, f32[32]{0:T(128)}, u32[]{:S(2)}) copy-start(f32[32]{0:T(128)} %constant.106.clone.1) | copy-start | bytes 388
  91.0 8.8 %copy-start.2 = (f32[8,16,128]{2,1,0:T(8,128)S(1)}, f32[8,16,128]{2,1,0:T(8,128)}, u32[]{:S(2)}) copy-start(f32[8,16,128]{2,1,0:T(8,128)} %param.14) | copy-start | bytes 196612
  91.0 8.8 %copy-start.5 = (s32[16,128]{1,0:T(8,128)S(1)}, s32[16,128]{1,0:T(8,128)}, u32[]{:S(2)}) copy-start(s32[16,128]{1,0:T(8,128)} %param.15) | copy-start | bytes 24580
  91.8 7.6 %collective-permute-start.3 = (f32[32,1,130]{2,0,1:T(8,128)}, f32[32,1,130]{2,0,1:T(8,128)S(1)}, u32[]{:S(2)}, u32[]{:S(2)}) collective-permute-start(f32[32,1,130]{2,0,1:T(8,128)} %get-tuple-element.19), channel_id=1, source_target_pairs={{1,0},{2,1},{3,2},{4,3},{5,4},{6,5},{7,6},{8,7},{9,8},{10,9},{11,1... | collective-permute-start | bytes 49928 | tf_op jit(solution)/shard_map/ppermute | solution.py:22
  102.5 72.2 %collective-permute-start.4 = (f32[32,16,1]{2,0,1:T(8,128)}, f32[32,16,1]{2,0,1:T(8,128)S(1)}, u32[]{:S(2)}, u32[]{:S(2)}) collective-permute-start(f32[32,16,1]{2,0,1:T(8,128)} %get-tuple-element.29), channel_id=1, source_target_pairs={{0,16},{16,32},{32,48},{48,64},{64,80},{80,96},{96,112},{112,128},... | collective-permute-start | bytes 6152 | tf_op jit(solution)/shard_map/ppermute | solution.py:20
  104.4 70.3 %collective-permute-start.5 = (f32[32,16,1]{2,0,1:T(8,128)}, f32[32,16,1]{2,0,1:T(8,128)S(1)}, u32[]{:S(2)}, u32[]{:S(2)}) collective-permute-start(f32[32,16,1]{2,0,1:T(8,128)} %get-tuple-element.30), channel_id=1, source_target_pairs={{16,0},{32,16},{48,32},{64,48},{80,64},{96,80},{112,96},{128,112},... | collective-permute-start | bytes 6152 | tf_op jit(solution)/shard_map/ppermute | solution.py:22
  174.8 17.2 %collective-permute-start.7 = (f32[32,1,130]{2,0,1:T(8,128)S(1)}, f32[32,1,130]{2,0,1:T(8,128)S(1)}, u32[]{:S(2)}, u32[]{:S(2)}) collective-permute-start(f32[32,1,130]{2,0,1:T(8,128)S(1)} %get-tuple-element.17), channel_id=1, source_target_pairs={{1,0},{2,1},{3,2},{4,3},{5,4},{6,5},{7,6},{8,7},{9,8},{10,9},{11,1... | collective-permute-start | bytes 49928 | tf_op jit(solution)/shard_map/ppermute | solution.py:22
  183.4 8.6 %collective-permute-start.6 = (f32[32,1,130]{2,0,1:T(8,128)S(1)}, f32[32,1,130]{2,0,1:T(8,128)S(1)}, u32[]{:S(2)}, u32[]{:S(2)}) collective-permute-start(f32[32,1,130]{2,0,1:T(8,128)S(1)} %get-tuple-element.18), channel_id=1, source_target_pairs={{0,1},{1,2},{2,3},{3,4},{4,5},{5,6},{6,7},{7,8},{8,9},{9,10},{10,1... | collective-permute-start | bytes 49928 | tf_op jit(solution)/shard_map/ppermute | solution.py:20
  186.1 6.3 %copy-start.4 = (f32[32,16,129]{2,0,1:T(8,128)S(1)}, f32[32,16,129]{2,0,1:T(8,128)}, u32[]{:S(2)}) copy-start(f32[32,16,129]{2,0,1:T(8,128)} %constant_dynamic-update-slice_fusion) | copy-start | bytes 792580
  192.9 5.9 %copy-start.11 = (bf16[9,64,24]{1,2,0:T(8,128)(2,1)S(1)}, bf16[9,64,24]{1,2,0:T(8,128)(2,1)}, u32[]{:S(2)}) copy-start(bf16[9,64,24]{1,2,0:T(8,128)(2,1)} %param.17) | copy-start | bytes 82948
  193.3 6.5 %collective-permute-start.8 = (bf16[40,16,1]{2,0,1:T(8,128)(2,1)S(1)}, bf16[40,16,1]{2,0,1:T(8,128)(2,1)S(1)}, u32[]{:S(2)}, u32[]{:S(2)}) collective-permute-start(bf16[40,16,1]{2,0,1:T(8,128)(2,1)S(1)} %get-tuple-element.35), channel_id=1, source_target_pairs={{0,16},{16,32},{32,48},{48,64},{64,80},{80,96},{96,112},{112,128},... | collective-permute-start | bytes 3848 | tf_op jit(solution)/shard_map/ppermute | solution.py:20
  195.3 6.6 %collective-permute-start.9 = (bf16[40,16,1]{2,0,1:T(8,128)(2,1)S(1)}, bf16[40,16,1]{2,0,1:T(8,128)(2,1)S(1)}, u32[]{:S(2)}, u32[]{:S(2)}) collective-permute-start(bf16[40,16,1]{2,0,1:T(8,128)(2,1)S(1)} %get-tuple-element.36), channel_id=1, source_target_pairs={{16,0},{32,16},{48,32},{64,48},{80,64},{96,80},{112,96},{128,112},... | collective-permute-start | bytes 3848 | tf_op jit(solution)/shard_map/ppermute | solution.py:22
  202.0 5.5 collective-permute-start.11
  204.0 8.4 %collective-permute-start.10 = (bf16[40,1,130]{2,0,1:T(8,128)(2,1)S(1)}, bf16[40,1,130]{2,0,1:T(8,128)(2,1)S(1)}, u32[]{:S(2)}, u32[]{:S(2)}) collective-permute-start(bf16[40,1,130]{2,0,1:T(8,128)(2,1)S(1)} %get-tuple-element.23), channel_id=1, source_target_pairs={{0,1},{1,2},{2,3},{3,4},{4,5},{5,6},{6,7},{7,8},{8,9},{9,10},{10,1... | collective-permute-start | bytes 31208 | tf_op jit(solution)/shard_map/ppermute | solution.py:20
  216.4 1.1 copy-start.3
  220.7 12.6 %collective-permute-start.12 = (bf16[64,16,1]{2,0,1:T(8,128)(2,1)S(1)}, bf16[64,16,1]{2,0,1:T(8,128)(2,1)S(1)}, u32[]{:S(2)}, u32[]{:S(2)}) collective-permute-start(bf16[64,16,1]{2,0,1:T(8,128)(2,1)S(1)} %get-tuple-element.25), channel_id=1, source_target_pairs={{0,16},{16,32},{32,48},{48,64},{64,80},{80,96},{96,112},{112,128},... | collective-permute-start | bytes 6152 | tf_op jit(solution)/shard_map/ppermute | solution.py:20
  223.9 10.3 %collective-permute-start.13 = (bf16[64,16,1]{2,0,1:T(8,128)(2,1)S(1)}, bf16[64,16,1]{2,0,1:T(8,128)(2,1)S(1)}, u32[]{:S(2)}, u32[]{:S(2)}) collective-permute-start(bf16[64,16,1]{2,0,1:T(8,128)(2,1)S(1)} %get-tuple-element.26), channel_id=1, source_target_pairs={{16,0},{32,16},{48,32},{64,48},{80,64},{96,80},{112,96},{128,112},... | collective-permute-start | bytes 6152 | tf_op jit(solution)/shard_map/ppermute | solution.py:22
  234.3 6.1 %collective-permute-start.15 = (bf16[64,1,130]{2,0,1:T(8,128)(2,1)S(1)}, bf16[64,1,130]{2,0,1:T(8,128)(2,1)S(1)}, u32[]{:S(2)}, u32[]{:S(2)}) collective-permute-start(bf16[64,1,130]{2,0,1:T(8,128)(2,1)S(1)} %get-tuple-element.16), channel_id=1, source_target_pairs={{1,0},{2,1},{3,2},{4,3},{5,4},{6,5},{7,6},{8,7},{9,8},{10,9},{11,1... | collective-permute-start | bytes 49928 | tf_op jit(solution)/shard_map/ppermute | solution.py:22
  236.9 8.6 %collective-permute-start.14 = (bf16[64,1,130]{2,0,1:T(8,128)(2,1)S(1)}, bf16[64,1,130]{2,0,1:T(8,128)(2,1)S(1)}, u32[]{:S(2)}, u32[]{:S(2)}) collective-permute-start(bf16[64,1,130]{2,0,1:T(8,128)(2,1)S(1)} %get-tuple-element.15), channel_id=1, source_target_pairs={{0,1},{1,2},{2,3},{3,4},{4,5},{5,6},{6,7},{7,8},{8,9},{9,10},{10,1... | collective-permute-start | bytes 49928 | tf_op jit(solution)/shard_map/ppermute | solution.py:20
  250.0 266.9 %copy-start.9 = (s32[8192]{0:T(1024)S(1)}, s32[8192]{0:T(1024)}, u32[]{:S(2)}) copy-start(s32[8192]{0:T(1024)} %fusion.151) | copy-start | bytes 98308
  251.5 303.0 %copy-start.8 = (s32[8192]{0:T(1024)S(1)}, s32[8192]{0:T(1024)}, u32[]{:S(2)}) copy-start(s32[8192]{0:T(1024)} %param.21) | copy-start | bytes 98308
Sparse Core Ops, SparseCore 0:
  249.5 267.4 all-reduce.1
where the time goes:
time: 563 us; the launch traced here: 562 us
  waiting for transfers between devices  286 us (51%)
  blocking collectives  128 us (23%)
  starting transfers between devices  64.2 us (11%)
  local copies, waits for them, and re-layouts  47.3 us (8%)
  between operations  14.8 us (3%)
  matrix products  13.1 us (2%)
  other arithmetic  9.02 us (2%)
    psum x1, waiting for transfers between devices, on_device(): grad_active = jnp.take(lax.psum(flat, ('lon', 'lat')), active_index)  265 us
    all_gather x2, blocking collectives, on_device(): lax.all_gather(source[:, row_count - 1:, :], 'lon', axis=2, tiled=True)  128 us
    ppermute x8, starting transfers between devices, padded_2(): lax.ppermute(head, axis, [((i + 1) % count, i) for i in range(count)])  40.8 us
    gather x1, local copies, waits for them, and re-layouts, on_device(): grad_active = jnp.take(lax.psum(flat, ('lon', 'lat')), active_index)  37.5 us
    ppermute x8, starting transfers between devices, padded_2(): lax.ppermute(tail, axis, [(i, (i + 1) % count) for i in range(count)])  23.3 us
    ppermute x8, waiting for transfers between devices, padded_2(): lax.ppermute(tail, axis, [(i, (i + 1) % count) for i in range(count)])  15.9 us
  transfers between devices with their start and end apart: 17, of which 7 were waited for; matrix products, arithmetic and copies ran while one was open for 2% of the time, Pallas kernels for 0%

commit v1 on v0

v1 whole, which is shorter than its diff:
```python
import collections
import functools
import math

import jax
import jax.numpy as jnp
import numpy as np
from jax import lax
from jax.experimental import pallas as pl
from jax.experimental.pallas import tpu as pltpu
from jax.sharding import PartitionSpec as P

coriolis_peak = 0.25
pressure_scale = 0.05
advect_scale = 0.25

LEV = 8
ROWS = 16
COLS = 128
HALO = 4
EXT = ROWS + 2 * HALO
WIDE = 2 * COLS
CH = 64
INS = 3 * LEV
OUTS = 2 * LEV
PACK = 48
TAPK = 80
FIRST = 9 * CH * INS
MIX = CH * CH
BOTH = ("lon", "lat")
F32 = jnp.float32
BF16 = jnp.bfloat16


def params(mib=48):
    return pltpu.CompilerParams(vmem_limit_bytes=mib * 1024 * 1024)


def vmem(count):
    return [pl.BlockSpec(memory_space=pltpu.VMEM)] * count


def smem():
    return pl.BlockSpec(memory_space=pltpu.SMEM)


def iota(shape, axis):
    return lax.broadcasted_iota(jnp.int32, shape, axis)


def prep_kernel(grad_scale, state, kappa, depth, cot, own, grad, top, bottom, edges):
    level = iota((LEV, COLS), 0)
    lane = iota((PACK, COLS), 1)
    fields = [jnp.swapaxes(state[f], 0, 1) for f in range(3)]
    kap = jnp.swapaxes(kappa[...], 0, 1)
    cots = jnp.swapaxes(cot[...].astype(F32), 0, 1)
    packed = jnp.zeros((PACK, COLS), F32)
    for r in range(ROWS):
        mask = (level < depth[r : r + 1, :]).astype(F32)
        row = jnp.concatenate([fields[f][r] * mask for f in range(3)] + [kap[r] * mask], axis=0)
        out_grad = grad_scale * jnp.concatenate([mask, mask], axis=0) * cots[r]
        own[r] = row
        grad[r] = out_grad.astype(BF16)
        both = jnp.concatenate([row, out_grad], axis=0)
        if r < HALO:
            bottom[r] = both.astype(BF16)
        if r >= ROWS - HALO:
            top[r - (ROWS - HALO)] = both.astype(BF16)
        moved = pltpu.roll(both, 8 * r, 1) if r else both
        here = ((lane - 8 * r + 4 + COLS) & (COLS - 1)) < 8
        packed = jnp.where(here, moved, packed)
    edges[...] = packed.astype(BF16)


def mid_kernel(scal, own_top, own_bottom, ra, rb, pla, plb, f1, f2, corner):
    core, rel, even = scal[0], scal[1], scal[2]
    lane = iota((PACK, COLS), 1)
    first_core = core == 0
    ea, eb = ra[HALO].astype(F32), rb[HALO].astype(F32)
    east_edge = jnp.where(first_core, ea, eb)
    west_edge = jnp.where(first_core, eb, ea)
    ce = jnp.where((lane & 7) < 4, east_edge, west_edge).astype(BF16)
    corner[...] = ce
    is_even = even == 1
    for k in range(HALO):
        up, down = own_top[k].astype(F32), own_bottom[k].astype(F32)
        pla[k] = jnp.where(is_even, up, down).astype(BF16)
        plb[k] = jnp.where(is_even, down, up).astype(BF16)
    pla[HALO] = ce
    plb[HALO] = ce
    rows_a = ra[:HALO].astype(F32).reshape(HALO * PACK, COLS)
    rows_b = rb[:HALO].astype(F32).reshape(HALO * PACK, COLS)
    west = jnp.where(first_core, rows_b, rows_a).astype(BF16)
    east = jnp.where(first_core, rows_a, rows_b).astype(BF16)
    window = jnp.concatenate([west, own_top[...].reshape(HALO * PACK, COLS), east], axis=1)
    src = iota((3 * COLS, WIDE), 0) - COLS
    t = iota((3 * COLS, WIDE), 1)
    q = t & 7
    target = jnp.where(t < COLS, t, jnp.where(q < 4, COLS + q, q - 8))
    chan = iota((PACK, COLS), 0)
    sign = jnp.where(chan < 2 * LEV, -1.0, jnp.where(chan < 4 * LEV, 1.0, 0.0)).astype(F32)
    slot = ((lane + 4) >> 3) & (ROWS - 1)
    for out, offset, least in ((f1, 0, -COLS), (f2, WIDE, 0)):
        pick = (src == rel - offset - target) & (src >= least)
        moved = jnp.dot(window, pick.astype(F32).astype(BF16), preferred_element_type=F32)
        ext = jnp.zeros((PACK, COLS), F32)
        for k in range(HALO):
            at = (HALO - 1 - k) * PACK
            out[k] = (moved[at : at + PACK, :COLS] * sign).astype(BF16)
            ext = jnp.where(slot == k, moved[at : at + PACK, COLS:], ext)
        out[HALO] = (ext * sign).astype(BF16)


def sigmoid(x):
    return 1.0 / (1.0 + jnp.exp(-x))


def main_kernel(
    scal, spin, valid, own, grad, ce, rla, rlb, rf1, rf2, w1, wm, wmt, wl, wb, hi, lo,
    state_out, closure_out, active_out,
    z0, z1, kxe, kxn, pres, gx, x3, g3, ybuf, acc_first, acc_rest, picked,
):
    even, top = scal[2] == 1, scal[3] == 1

    def place(y, left, corner_pack, slot):
        shift = (COLS - 8 * slot) % COLS
        right = pltpu.roll(corner_pack, shift, 1) if shift else corner_pack
        z0[y, :, :COLS] = left[: 4 * LEV]
        z0[y, :, COLS:] = right[: 4 * LEV]
        gx[y, :, :COLS] = left[4 * LEV :]
        gx[y, :, COLS:] = right[4 * LEV :]

    def south(k):
        return jnp.where(even, rlb[k].astype(F32), rla[k].astype(F32))

    def north(k):
        near = jnp.where(even, rla[k].astype(F32), rlb[k].astype(F32))
        return jnp.where(top, rf1[k].astype(F32) + rf2[k].astype(F32), near)

    south_edge, north_edge, own_edge = south(HALO), north(HALO), ce[...].astype(F32)
    for k in range(HALO):
        place(k, south(k), south_edge, ROWS - HALO + k)
        place(HALO + ROWS + k, north(k), north_edge, k)
    for r in range(ROWS):
        full = jnp.concatenate([own[r], grad[r].astype(F32)], axis=0)
        place(HALO + r, full, own_edge, r)

    def east(x):
        return pltpu.roll(x, WIDE - 1, 1)

    def west(x):
        return pltpu.roll(x, 1, 1)

    level = iota((LEV, WIDE), 0)

    def depth_sum(x):
        for s in (1, 2, 4):
            x = x + jnp.where(level >= s, pltpu.roll(x, s, 0), 0.0)
        return x

    U, V, T, K = (slice(LEV * i, LEV * (i + 1)) for i in range(4))

    def coefficients(y, _):
        k = z0[y, K]
        kxe[y] = jnp.sqrt(k * east(k))
        kxn[y] = jnp.sqrt(k * z0[jnp.minimum(y + 1, EXT - 1), K])
        pres[y] = pressure_scale * depth_sum(z0[y, T])
        return 0

    lax.fori_loop(0, EXT, coefficients, 0, unroll=4)

    def step(src, dst, y):
        ke, kn, ks = kxe[y], kxn[y], kxn[y - 1]
        u, v, t = src[y, U], src[y, V], src[y, T]
        wet = (z0[y, K] > 0).astype(F32)
        f = spin[y]

        def diffuse(z, zn, zs):
            flux = ke * (east(z) - z)
            return flux - west(flux) + kn * (zn - z) + ks * (zs - z)

        p = pres[y]
        un, us = src[y + 1, U], src[y - 1, U]
        vn, vs = src[y + 1, V], src[y - 1, V]
        tn, ts = src[y + 1, T], src[y - 1, T]
        du = f * v - 0.5 * (east(p) - west(p))
        dv = -f * u - 0.5 * (pres[y + 1] - pres[y - 1])
        dt = (-advect_scale * 0.5) * (u * (east(t) - west(t)) + v * (tn - ts))
        dst[y, U] = wet * (u + du + diffuse(u, un, us))
        dst[y, V] = wet * (v + dv + diffuse(v, vn, vs))
        dst[y, T] = wet * (t + dt + diffuse(t, tn, ts))

    def first_step(i, _):
        step(z0, z1, i)
        return 0

    lax.fori_loop(1, EXT - 1, first_step, 0, unroll=2)

    def second_pressure(y, _):
        pres[y] = pressure_scale * depth_sum(z1[y, T])
        return 0

    lax.fori_loop(1, EXT - 1, second_pressure, 0, unroll=2)

    zero_rows = jnp.zeros((TAPK - 3 * INS, WIDE), F32)

    def second_step(y, _):
        step(z1, z0, y)
        x = z0[y, :INS] * valid[y]
        taps = jnp.concatenate([west(x), x, east(x), zero_rows], axis=0)
        x3[pl.ds(pl.multiple_of(TAPK * y, 16), TAPK), :] = taps.astype(BF16)
        g = gx[y]
        tap_g = jnp.concatenate([east(g), g, west(g)], axis=0)[:, :COLS]
        g3[pl.ds(pl.multiple_of(PACK * y, 16), PACK), :] = tap_g.astype(BF16)
        return 0

    lax.fori_loop(2, EXT - 2, second_step, 0, unroll=2)
    new = z0[HALO : HALO + ROWS, :INS, :COLS]
    for f in range(3):
        state_out[f] = jnp.swapaxes(new[:, LEV * f : LEV * (f + 1), :], 0, 1)

    def forward(y):
        taps = x3[pl.ds(pl.multiple_of(TAPK * (y - 1), 16), 3 * TAPK), :]
        pre1 = jnp.dot(w1[...], taps, preferred_element_type=F32)
        s1 = sigmoid(pre1)
        h1 = (pre1 * s1).astype(BF16)
        pre2 = jnp.dot(wm[...], h1, preferred_element_type=F32)
        s2 = sigmoid(pre2)
        h2 = (pre2 * s2 * valid[y]).astype(BF16)
        ybuf[y] = jnp.dot(wl[...], h2, preferred_element_type=F32)
        return taps, pre1, s1, h1, pre2, s2, h2

    forward(HALO - 1)
    forward(HALO + ROWS)
    acc_first[...] = jnp.zeros_like(acc_first)
    acc_rest[...] = jnp.zeros_like(acc_rest)
    nt = (((1,), (1,)), ((), ()))

    def both_ways(i, _):
        y = HALO + i
        taps, pre1, s1, h1, pre2, s2, h2 = (x[:, :COLS] for x in forward(y))
        g9 = g3[pl.ds(pl.multiple_of(PACK * (y - 1), 16), 3 * PACK), :]
        back2 = jnp.dot(wb[...], g9, preferred_element_type=F32)
        d2 = (back2 * (s2 * (1.0 + pre2 * (1.0 - s2)))).astype(BF16)
        back1 = jnp.dot(wmt[...], d2, preferred_element_type=F32)
        d1 = (back1 * (s1 * (1.0 + pre1 * (1.0 - s1)))).astype(BF16)
        acc_first[:, : 3 * TAPK] += lax.dot_general(d1, taps, nt, preferred_element_type=F32)
        gap = jnp.zeros((16, COLS), BF16)
        right = jnp.concatenate([jnp.zeros((160, COLS), BF16), h1, jnp.zeros((32, COLS), BF16)], axis=0)
        left = jnp.concatenate([g9, gap, jnp.zeros((96, COLS), BF16)], axis=0)
        acc_rest[...] += lax.dot_general(h2, left, nt, preferred_element_type=F32) + lax.dot_general(
            d2, right, nt, preferred_element_type=F32
        )
        return 0

    lax.fori_loop(0, ROWS, both_ways, 0)

    closed = []
    for r in range(ROWS):
        y = HALO + r
        part = [
            ybuf[y - 1, OUTS * d : OUTS * (d + 1)]
            + ybuf[y, OUTS * (3 + d) : OUTS * (4 + d)]
            + ybuf[y + 1, OUTS * (6 + d) : OUTS * (7 + d)]
            for d in range(3)
        ]
        total = (west(part[0]) + part[1] + east(part[2]))[:, :COLS]
        wet = (own[r, K] > 0).astype(F32)
        closed.append(jnp.concatenate([wet, wet], axis=0) * total)
    closure_out[...] = jnp.swapaxes(jnp.stack(closed), 0, 1).astype(BF16)

    table = jnp.concatenate([acc_first[...], acc_rest[...]], axis=0).astype(BF16)
    column = iota((WIDE, WIDE), 0)
    line = iota((2 * CH, WIDE), 0)

    def choose(c, _):
        at_hi = jnp.concatenate([hi[pl.ds(2 * c, 1), :], hi[pl.ds(2 * c + 1, 1), :]], axis=1)
        at_lo = jnp.concatenate([lo[pl.ds(2 * c, 1), :], lo[pl.ds(2 * c + 1, 1), :]], axis=1)
        hot = (column == at_hi).astype(F32).astype(BF16)
        found = jnp.dot(table, hot, preferred_element_type=F32)
        value = jnp.sum(jnp.where(line == at_lo, found, 0.0), axis=0, keepdims=True)
        picked[pl.ds(2 * c, 1), :] = value[:, :COLS]
        picked[pl.ds(2 * c + 1, 1), :] = value[:, COLS:]
        return 0

    lax.fori_loop(0, hi.shape[0] // 2, choose, 0, unroll=2)
    active_out[...] = picked[...].astype(BF16)


def swap_pairs(count, start):
    out = []
    for i in range(start, count - 1 + start, 2):
        a, b = i % count, (i + 1) % count
        out += [(a, b), (b, a)]
    return out


def fold_pairs(lon_count, lat_count, q):
    row = lat_count - 1
    return [(i * lat_count + row, ((2 * q - i) % lon_count) * lat_count + row) for i in range(lon_count)]


def groups_of(count, key):
    out = collections.OrderedDict()
    for i in range(count):
        out.setdefault(key(i), []).append(i)
    return list(out.values())


def reduce_over(x, axis, groups):
    count = len(groups[0])
    y = jnp.broadcast_to(x.astype(BF16)[None], (count,) + x.shape)
    y = lax.all_to_all(y, axis, 0, 0, axis_index_groups=groups)
    return jnp.sum(y.astype(F32), axis=0)


def placed_entries(active_index):
    n = active_index
    k, rem = n // (CH * INS), n % (CH * INS)
    hi_a, lo_a = (k // 3) * TAPK + (k % 3) * INS + rem % INS, rem // INS
    g = n - FIRST
    hi_b, lo_b = 160 + g % CH, CH + g // CH
    g = n - FIRST - MIX
    k, rem = g // (OUTS * CH), g % (OUTS * CH)
    hi_c, lo_c = (2 - k // 3) * PACK + (k % 3) * OUTS + rem // CH, CH + rem % CH
    in_a, in_b = n < FIRST, n < FIRST + MIX
    hi = jnp.where(in_a, hi_a, jnp.where(in_b, hi_b, hi_c))
    lo = jnp.where(in_a, lo_a, jnp.where(in_b, lo_b, lo_c))
    return hi.reshape(-1, COLS), lo.reshape(-1, COLS)


def on_device(
    lon_count, lat_count,
    ocean_state, diffusivity, depth_levels, fold_pair, first_weight, mix_weight, last_weight, cotangent, active_index,
):
    lat, lon = lax.axis_index("lat"), lax.axis_index("lon")
    row_total, col_total = ROWS * lat_count, COLS * lon_count
    shape = jax.ShapeDtypeStruct
    own, grad, top, bottom, edges = pl.pallas_call(
        functools.partial(prep_kernel, 1.0 / math.sqrt(row_total * col_total)),
        out_shape=(
            shape((ROWS, 4 * LEV, COLS), F32),
            shape((ROWS, OUTS, COLS), BF16),
            shape((HALO, PACK, COLS), BF16),
            shape((HALO, PACK, COLS), BF16),
            shape((PACK, COLS), BF16),
        ),
        in_specs=vmem(4),
        out_specs=tuple(vmem(5)),
        compiler_params=params(),
        name="prep",
    )(ocean_state, diffusivity, depth_levels, cotangent)

    send = jnp.concatenate([top, edges[None]], axis=0)
    ra = lax.ppermute(send, "lon", swap_pairs(lon_count, 0))
    rb = lax.ppermute(send, "lon", swap_pairs(lon_count, 1) )

    folded = (fold_pair[0] - 3) % col_total
    turn, rel = folded // WIDE, folded % WIDE + 3
    twice = (rel + 4 >= WIDE).astype(jnp.int32)
    scal = jnp.stack(
        [lon % 2, rel, (lat % 2 == 0).astype(jnp.int32), (lat == lat_count - 1).astype(jnp.int32)]
    ).astype(jnp.int32)
    ext_rows = lat * ROWS - HALO + jnp.arange(EXT, dtype=jnp.int32)
    mirrored = jnp.where(ext_rows >= row_total, 2 * row_total - 1 - ext_rows, ext_rows)
    spin = coriolis_peak * jnp.sin(math.pi * (mirrored.astype(F32) + 0.5) / row_total - 0.5 * math.pi)
    valid = ((ext_rows >= 0) & (ext_rows < row_total)).astype(F32)
    hi, lo = placed_entries(active_index)
    w1 = jnp.pad(
        first_weight.reshape(3, 3, CH, INS).transpose(2, 0, 1, 3).reshape(CH, 3, 3 * INS),
        ((0, 0), (0, 0), (0, TAPK - 3 * INS)),
    ).reshape(CH, 3 * TAPK)
    wl = last_weight.reshape(9 * OUTS, CH)
    wb = last_weight.reshape(3, 3, OUTS, CH)[::-1].reshape(9 * OUTS, CH).T
    wmt = mix_weight.T

    block = shape((HALO + 1, PACK, COLS), BF16)
    pla, plb, f1, f2, ce = pl.pallas_call(
        mid_kernel,
        out_shape=(block, block, block, block, shape((PACK, COLS), BF16)),
        in_specs=[smem()] + vmem(4),
        out_specs=tuple(vmem(5)),
        compiler_params=params(),
        name="mid",
    )(scal, top, bottom, ra, rb)

    near_a = swap_pairs(lat_count, 0)
    near_b = swap_pairs(lat_count - 1, 1)

    def exchange(q, second):
        def run(pla, plb, f1, f2):
            rf1 = lax.ppermute(f1, BOTH, fold_pairs(lon_count, lat_count, q))
            if second:
                rf2 = lax.ppermute(f2, BOTH, fold_pairs(lon_count, lat_count, q + 1))
            else:
                rf2 = jnp.zeros_like(f2)
            return lax.ppermute(pla, "lat", near_a), lax.ppermute(plb, "lat", near_b), rf1, rf2

        return run

    turns = lon_count // 2
    branches = [exchange(q, second) for q in range(turns) for second in (False, True)]
    rla, rlb, rf1, rf2 = lax.switch(2 * turn + twice, branches, pla, plb, f1, f2)

    lines = active_index.shape[0] // COLS
    new_state, closure, active = pl.pallas_call(
        main_kernel,
        out_shape=(
            shape((3, LEV, ROWS, COLS), F32),
            shape((OUTS, ROWS, COLS), BF16),
            shape((lines, COLS), BF16),
        ),
        in_specs=[smem()] * 3 + vmem(14),
        out_specs=tuple(vmem(3)),
        scratch_shapes=[
            pltpu.VMEM((EXT, 4 * LEV, WIDE), F32),
            pltpu.VMEM((EXT, 4 * LEV, WIDE), F32),
            pltpu.VMEM((EXT, LEV, WIDE), F32),
            pltpu.VMEM((EXT, LEV, WIDE), F32),
            pltpu.VMEM((EXT, LEV, WIDE), F32),
            pltpu.VMEM((EXT, OUTS, WIDE), F32),
            pltpu.VMEM((EXT * TAPK, WIDE), BF16),
            pltpu.VMEM((EXT * PACK, COLS), BF16),
            pltpu.VMEM((EXT, 9 * OUTS, WIDE), F32),
            pltpu.VMEM((CH, WIDE), F32),
            pltpu.VMEM((CH, WIDE), F32),
            pltpu.VMEM((lines, COLS), F32),
        ],
        compiler_params=params(),
        name="main",
    )(scal, spin, valid, own, grad, ce, rla, rlb, rf1, rf2, w1, mix_weight, wmt, wl, wb, hi, lo)

    total = reduce_over(active, "lat", groups_of(lat_count, lambda i: 0))
    total = reduce_over(total, "lon", groups_of(lon_count, lambda i: i // 16))
    mine = total.astype(BF16)
    half = lon_count // 2
    other = lax.ppermute(mine, "lon", [(i, (i + half) % lon_count) for i in range(lon_count)])
    total = mine.astype(F32) + other.astype(F32)
    return new_state, closure, total.reshape(-1)


def solution(mesh):
    in_specs = (
        P(None, None, "lat", "lon"),
        P(None, "lat", "lon"),
        P("lat", "lon"),
        P(),
        P(),
        P(),
        P(),
        P(None, "lat", "lon"),
        P(),
    )
    out_specs = (P(None, None, "lat", "lon"), P(None, "lat", "lon"), P())
    body = functools.partial(on_device, mesh.shape["lon"], mesh.shape["lat"])
    return jax.shard_map(body, mesh=mesh, in_specs=in_specs, out_specs=out_specs, check_vma=False)
```

time: 563 us -> 103 us (0.18)
  waiting for transfers between devices: 286 us -> 1.73 us
  blocking collectives: 128 us -> 46.2 us
  starting transfers between devices: 64.2 us -> 23.2 us
  local copies, waits for them, and re-layouts: 47.3 us -> 7.41 us
  Pallas kernels: 0 us -> 21.2 us
  between operations: 14.8 us -> 1.53 us
  matrix products: 13.1 us -> 0 us
  other arithmetic: 9.02 us -> 1.09 us
    psum x1 -> x0, waiting for transfers between devices: 265 us -> none  [on_device(): grad_active = jnp.take(lax.psum(flat, ('lon', 'lat')), active_index)]
    all_gather x2 -> x0, blocking collectives: 128 us -> none  [on_device(): lax.all_gather(source[:, row_count - 1:, :], 'lon', axis=2, tiled=True)]
    all_to_all x0 -> x2, blocking collectives: none -> 46.2 us  [reduce_over(): y = lax.all_to_all(y, axis, 0, 0, axis_index_groups=groups)]
    ppermute x16 -> x6, starting transfers between devices: 64.2 us -> 23.2 us  [the longest x1 8.79 us: on_device(): ra = lax.ppermute(send, 'lon', swap_pairs(lon_count, 0))]
    gather x6 -> x0, local copies, waits for them, and re-layouts: 40.4 us -> none  [the longest x1 37.5 us: on_device(): grad_active = jnp.take(lax.psum(flat, ('lon', 'lat')), active_index)]
    pallas_call x0 -> x3, Pallas kernels: none -> 21.2 us  [the longest x1 20.2 us: on_device(): pl.pallas_call(main_kernel, out_shape=(shape((3, LEV, ROWS, COLS), F32),...]
    ppermute x16 -> x6, waiting for transfers between devices: 20.2 us -> 1.73 us  [the longest x1 1.16 us: on_device(): lax.ppermute(mine, 'lon', [(i, (i + half) % lon_count) for i in range(lon...]
    dot_general x48 -> x0, matrix products: 13.1 us -> none  [the longest x18 4.73 us: convolve(): jnp.einsum('oc,cyx->oyx', weight[tap_index], padded[:, tap_row:tap_row +...]
  transfers between devices with their start and end apart: 17 -> 6, of which waited for: 7 -> 2; matrix products, arithmetic and copies ran while one was open for 2% -> 2% of each run, Pallas kernels for 0% -> 0%
where the time goes in v1:
time: 103 us; the launch traced here: 102 us
  blocking collectives  46.2 us (45%)
  starting transfers between devices  23.2 us (23%)
  Pallas kernels  21.2 us (21%)
  local copies, waits for them, and re-layouts  7.41 us (7%)
  waiting for transfers between devices  1.73 us (2%)
  between operations  1.53 us (1%)
  other arithmetic  1.09 us (1%)
    all_to_all x2, blocking collectives, reduce_over(): y = lax.all_to_all(y, axis, 0, 0, axis_index_groups=groups)  46.2 us
    pallas_call x1, Pallas kernels, on_device(): pl.pallas_call(main_kernel, out_shape=(shape((3, LEV, ROWS, COLS), F32),...  20.2 us
    ppermute x1, starting transfers between devices, on_device(): ra = lax.ppermute(send, 'lon', swap_pairs(lon_count, 0))  8.79 us
    ppermute x1, starting transfers between devices, on_device(): lax.ppermute(mine, 'lon', [(i, (i + half) % lon_count) for i in range(lon...  8.04 us
    unnamed x17, local copies, waits for them, and re-layouts  5.3 us
  transfers between devices with their start and end apart: 6, of which 2 were waited for; matrix products, arithmetic and copies ran while one was open for 2% of the time, Pallas kernels for 0%

profile of v1, /device:TPU:1, one launch (start us, length us, event | category | flops | bytes accessed | tf_op | source)
XLA Modules:
  0.0 102.5 jit_solution(13635036876462033861)
XLA Ops:
  0.6 0.0 copy-start
  0.6 0.9 copy-done
  1.6 0.0 copy-start.3
  1.6 0.8 copy-done.3
  2.4 0.0 copy-start.4
  2.4 0.8 copy-done.4
  3.2 0.0 copy-start.5
  3.2 0.7 copy-done.5
  3.9 0.2 prep.1
  4.1 8.8 %collective-permute-start.112 = (bf16[5,48,128]{2,1,0:T(8,128)(2,1)S(1)}, bf16[5,48,128]{2,1,0:T(8,128)(2,1)S(1)}, u32[]{:S(2)}, u32[]{:S(2)}) collective-permute-start(bf16[5,48,128]{2,1,0:T(8,128)(2,1)S(1)} %pad_maximum_fusion), channel_id=1, source_target_pairs={{0,16},{16,0},{32,48},{48,32},{64,80},{80,64},{96,112},{112,96},{1... | collective-permute-start | bytes 184328 | tf_op jit(solution)/shard_map/ppermute | solution.py:355
  12.9 1.9 %collective-permute-start.113 = (bf16[5,48,128]{2,1,0:T(8,128)(2,1)S(1)}, bf16[5,48,128]{2,1,0:T(8,128)(2,1)S(1)}, u32[]{:S(2)}, u32[]{:S(2)}) collective-permute-start(bf16[5,48,128]{2,1,0:T(8,128)(2,1)S(1)} %pad_maximum_fusion), channel_id=1, source_target_pairs={{16,32},{32,16},{48,64},{64,48},{80,96},{96,80},{112,128},{128,112... | collective-permute-start | bytes 184328 | tf_op jit(solution)/shard_map/ppermute | solution.py:356
  14.9 1.2 %slice.3 = s32[1]{0:T(128)} slice(s32[4096]{0:T(1024)} %param.44), slice={[0:1]} | slice | bytes 8 | tf_op jit(solution)/shard_map/slice | solution.py:358
  16.7 0.0 copy-start.7
  16.9 0.0 copy-start.6
  16.9 0.6 copy-done.7
  17.5 0.2 fusion.14
  17.7 0.0 copy-done.6
  17.8 0.0 copy-start.1
  17.8 0.1 copy.21.w1
  17.9 0.7 copy-done.1
  18.6 0.0 copy-start.2
  18.6 0.1 copy.20
  18.7 0.6 copy-done.2
  19.3 0.1 copy.19
  19.4 0.1 pad_add_fusion.scal
  19.5 0.0 collective-permute-done.112.ra
  19.5 0.0 collective-permute-done.113.rb
  19.5 0.8 mid.1
  20.3 5.7 %conditional.1 = (bf16[5,48,128]{2,1,0:T(8,128)(2,1)}, bf16[5,48,128]{2,1,0:T(8,128)(2,1)}, bf16[5,48,128]{2,1,0:T(8,128)(2,1)}, bf16[5,48,128]{2,1,0:T(8,128)(2,1)}) conditional(s32[]{:T(128)} %clamp.3, (bf16[5,48,128]{2,1,0:T(8,128)(2,1)S(1)}, bf16[5,48,128]{2,1,0:T(8,128)(2,1)S(1)}, ...), branch_computations={%region_0.1_spmd, %region_1.2_spmd, %region_2.3_spmd, %region_3.4_... | conditional | bytes 983232 | solution.py:403
  20.3 1.9 %collective-permute-start.7 = (bf16[5,48,128]{2,1,0:T(8,128)(2,1)S(1)}, bf16[5,48,128]{2,1,0:T(8,128)(2,1)}, u32[]{:S(2)}, u32[]{:S(2)}) collective-permute-start(bf16[5,48,128]{2,1,0:T(8,128)(2,1)S(1)} %get-tuple-element.231), channel_id=1, source_target_pairs={{0,1},{1,0},{2,3},{3,2},{4,5},{5,4},{6,7},{7,6},{8,9},{9,8},{10,11... | collective-permute-start | bytes 184328 | tf_op jit(solution)/shard_map/cond/branch_2_fun/ppermute | solution.py:397
  22.3 1.3 %collective-permute-start.8 = (bf16[5,48,128]{2,1,0:T(8,128)(2,1)S(1)}, bf16[5,48,128]{2,1,0:T(8,128)(2,1)}, u32[]{:S(2)}, u32[]{:S(2)}) collective-permute-start(bf16[5,48,128]{2,1,0:T(8,128)(2,1)S(1)} %get-tuple-element.232), channel_id=1, source_target_pairs={{1,2},{2,1},{3,4},{4,3},{5,6},{6,5},{7,8},{8,7},{9,10},{10,9},{11,... | collective-permute-start | bytes 184328 | tf_op jit(solution)/shard_map/cond/branch_2_fun/ppermute | solution.py:397
  23.6 1.3 %collective-permute-start.9 = (bf16[5,48,128]{2,1,0:T(8,128)(2,1)S(1)}, bf16[5,48,128]{2,1,0:T(8,128)(2,1)}, u32[]{:S(2)}, u32[]{:S(2)}) collective-permute-start(bf16[5,48,128]{2,1,0:T(8,128)(2,1)S(1)} %get-tuple-element.233), channel_id=1, source_target_pairs={{15,47},{31,31},{47,15},{63,511},{79,495},{95,479},{111,463},{127,... | collective-permute-start | bytes 184328 | tf_op jit(solution)/shard_map/cond/branch_2_fun/ppermute | solution.py:392
  24.9 0.6 collective-permute-done.7
  25.4 0.0 collective-permute-done.8
  25.4 0.0 collective-permute-done.9
  25.4 0.6 broadcast.97
  26.1 20.2 %main.1 = (f32[3,8,16,128]{3,2,1,0:T(8,128)}, bf16[16,16,128]{2,1,0:T(8,128)(2,1)}, bf16[64,128]{1,0:T(8,128)(2,1)S(1)}) custom-call(s32[4]{0:T(128)S(1)} %pad_add_fusion.scal, f32[24]{0:T(128)S(1)} %fusion.31.spin, f32[24]{0:T(128)S(1)} %and_convert_fusion.valid, f32[16,32,128]{2,1,0:T(8,128)S(1)} %get-tuple-element.356.own, ...), custom_call_target="tpu_custom_call" | custom-call | tf_op jit(solution)/shard_map/main/pallas_call | solution.py:406
  46.3 16.8 %all_to_all.10 = bf16[16,64,128]{2,1,0:T(8,128)(2,1)S(1)} all-to-all(bf16[16,64,128]{2,1,0:T(8,128)(2,1)S(1)} %broadcast_in_dim.7), channel_id=1, replica_groups={{0,1,2,3,4,5,6,7,8,9,10,11,12,13,14,15},{16,17,18,19,20,21,22,23,24,25,..., dimensions={0} | all-to-all | bytes 524288 | tf_op jit(solution)/shard_map/all_to_all | solution.py:313
  63.2 29.4 %all_to_all.11 = bf16[16,64,128]{2,1,0:T(8,128)(2,1)S(1)} all-to-all(bf16[16,64,128]{2,1,0:T(8,128)(2,1)S(1)} %broadcast_in_dim.8), channel_id=1, replica_groups={{0,16,32,48,64,80,96,112,128,144,160,176,192,208,224,240},{256,272,288,..., dimensions={0} | all-to-all | bytes 524288 | tf_op jit(solution)/shard_map/all_to_all | solution.py:313
  92.7 8.0 %collective-permute-start.114 = (bf16[64,128]{1,0:T(8,128)(2,1)S(1)}, bf16[64,128]{1,0:T(8,128)(2,1)S(1)}, u32[]{:S(2)}, u32[]{:S(2)}) collective-permute-start(bf16[64,128]{1,0:T(8,128)(2,1)S(1)} %reduce_sum.25), channel_id=1, source_target_pairs={{0,256},{16,272},{32,288},{48,304},{64,320},{80,336},{96,352},{112... | collective-permute-start | bytes 49160 | tf_op jit(solution)/shard_map/ppermute | solution.py:437
  100.7 1.2 %collective-permute-done.114 = bf16[64,128]{1,0:T(8,128)(2,1)S(1)} collective-permute-done((bf16[64,128]{1,0:T(8,128)(2,1)S(1)}, bf16[64,128]{1,0:T(8,128)(2,1)S(1)}, u32[]{:S(2)}, u32[]{:S(2)}) %collective-permute-start.114) | collective-permute-done | bytes 16416 | tf_op jit(solution)/shard_map/ppermute | solution.py:437
  101.9 0.6 add_bitcast_fusion
  (9 shorter events, 0.3 us)
Async XLA Ops:
  0.6 0.9 copy-start
  1.6 0.8 copy-start.3
  2.4 0.8 copy-start.4
  3.2 0.7 copy-start.5
  4.1 15.3 %collective-permute-start.112 = (bf16[5,48,128]{2,1,0:T(8,128)(2,1)S(1)}, bf16[5,48,128]{2,1,0:T(8,128)(2,1)S(1)}, u32[]{:S(2)}, u32[]{:S(2)}) collective-permute-start(bf16[5,48,128]{2,1,0:T(8,128)(2,1)S(1)} %pad_maximum_fusion), channel_id=1, source_target_pairs={{0,16},{16,0},{32,48},{48,32},{64,80},{80,64},{96,112},{112,96},{1... | collective-permute-start | bytes 184328 | tf_op jit(solution)/shard_map/ppermute | solution.py:355
  12.9 6.5 %collective-permute-start.113 = (bf16[5,48,128]{2,1,0:T(8,128)(2,1)S(1)}, bf16[5,48,128]{2,1,0:T(8,128)(2,1)S(1)}, u32[]{:S(2)}, u32[]{:S(2)}) collective-permute-start(bf16[5,48,128]{2,1,0:T(8,128)(2,1)S(1)} %pad_maximum_fusion), channel_id=1, source_target_pairs={{16,32},{32,16},{48,64},{64,48},{80,96},{96,80},{112,128},{128,112... | collective-permute-start | bytes 184328 | tf_op jit(solution)/shard_map/ppermute | solution.py:356
  16.7 0.8 copy-start.7
  16.9 0.9 copy-start.6
  17.8 0.8 copy-start.1
  18.6 0.7 copy-start.2
  20.3 5.1 %collective-permute-start.7 = (bf16[5,48,128]{2,1,0:T(8,128)(2,1)S(1)}, bf16[5,48,128]{2,1,0:T(8,128)(2,1)}, u32[]{:S(2)}, u32[]{:S(2)}) collective-permute-start(bf16[5,48,128]{2,1,0:T(8,128)(2,1)S(1)} %get-tuple-element.231), channel_id=1, source_target_pairs={{0,1},{1,0},{2,3},{3,2},{4,5},{5,4},{6,7},{7,6},{8,9},{9,8},{10,11... | collective-permute-start | bytes 184328 | tf_op jit(solution)/shard_map/cond/branch_2_fun/ppermute | solution.py:397
  22.3 3.1 %collective-permute-start.8 = (bf16[5,48,128]{2,1,0:T(8,128)(2,1)S(1)}, bf16[5,48,128]{2,1,0:T(8,128)(2,1)}, u32[]{:S(2)}, u32[]{:S(2)}) collective-permute-start(bf16[5,48,128]{2,1,0:T(8,128)(2,1)S(1)} %get-tuple-element.232), channel_id=1, source_target_pairs={{1,2},{2,1},{3,4},{4,3},{5,6},{6,5},{7,8},{8,7},{9,10},{10,9},{11,... | collective-permute-start | bytes 184328 | tf_op jit(solution)/shard_map/cond/branch_2_fun/ppermute | solution.py:397
  23.6 1.9 %collective-permute-start.9 = (bf16[5,48,128]{2,1,0:T(8,128)(2,1)S(1)}, bf16[5,48,128]{2,1,0:T(8,128)(2,1)}, u32[]{:S(2)}, u32[]{:S(2)}) collective-permute-start(bf16[5,48,128]{2,1,0:T(8,128)(2,1)S(1)} %get-tuple-element.233), channel_id=1, source_target_pairs={{15,47},{31,31},{47,15},{63,511},{79,495},{95,479},{111,463},{127,... | collective-permute-start | bytes 184328 | tf_op jit(solution)/shard_map/cond/branch_2_fun/ppermute | solution.py:392
  92.7 9.2 %collective-permute-start.114 = (bf16[64,128]{1,0:T(8,128)(2,1)S(1)}, bf16[64,128]{1,0:T(8,128)(2,1)S(1)}, u32[]{:S(2)}, u32[]{:S(2)}) collective-permute-start(bf16[64,128]{1,0:T(8,128)(2,1)S(1)} %reduce_sum.25), channel_id=1, source_target_pairs={{0,256},{16,272},{32,288},{48,304},{64,320},{80,336},{96,352},{112... | collective-permute-start | bytes 49160 | tf_op jit(solution)/shard_map/ppermute | solution.py:437

commit v2 on v1

--- a/solution.py
+++ b/solution.py
@@ -4,7 +4,6 @@
 
 import jax
 import jax.numpy as jnp
-import numpy as np
 from jax import lax
 from jax.experimental import pallas as pl
 from jax.experimental.pallas import tpu as pltpu
@@ -48,7 +47,15 @@
     return lax.broadcasted_iota(jnp.int32, shape, axis)
 
 
-def prep_kernel(grad_scale, state, kappa, depth, cot, own, grad, top, bottom, edges):
+def prep_kernel(
+    grad_scale, state_hbm, kappa_hbm, depth_hbm, cot_hbm, own, grad, send, bottom, state, kappa, depth, cot, sems
+):
+    pairs = ((state_hbm, state), (kappa_hbm, kappa), (depth_hbm, depth), (cot_hbm, cot))
+    copies = [pltpu.make_async_copy(a, b, sems.at[i]) for i, (a, b) in enumerate(pairs)]
+    for copy in copies:
+        copy.start()
+    for copy in copies:
+        copy.wait()
     level = iota((LEV, COLS), 0)
     lane = iota((PACK, COLS), 1)
     fields = [jnp.swapaxes(state[f], 0, 1) for f in range(3)]
@@ -65,15 +72,15 @@
         if r < HALO:
             bottom[r] = both.astype(BF16)
         if r >= ROWS - HALO:
-            top[r - (ROWS - HALO)] = both.astype(BF16)
+            send[r - (ROWS - HALO)] = both.astype(BF16)
         moved = pltpu.roll(both, 8 * r, 1) if r else both
         here = ((lane - 8 * r + 4 + COLS) & (COLS - 1)) < 8
         packed = jnp.where(here, moved, packed)
-    edges[...] = packed.astype(BF16)
-
-
-def mid_kernel(scal, own_top, own_bottom, ra, rb, pla, plb, f1, f2, corner):
-    core, rel, even = scal[0], scal[1], scal[2]
+    send[HALO] = packed.astype(BF16)
+
+
+def mid_kernel(scal, own_top, own_bottom, rb, ra, pla, plb, plc, corner):
+    core, rel, even, at_top = scal[0], scal[1], scal[2], scal[3] == 1
     lane = iota((PACK, COLS), 1)
     first_core = core == 0
     ea, eb = ra[HALO].astype(F32), rb[HALO].astype(F32)
@@ -88,11 +95,23 @@
         plb[k] = jnp.where(is_even, down, up).astype(BF16)
     pla[HALO] = ce
     plb[HALO] = ce
+
+    @pl.when(jnp.logical_not(at_top))
+    def _():
+        plc[...] = jnp.zeros_like(plc)
+
+    @pl.when(at_top)
+    def _():
+        fold_windows(first_core, rel, own_top, ra, rb, plb, plc)
+
+
+def fold_windows(first_core, rel, own_top, ra, rb, f1, f2):
+    lane = iota((PACK, COLS), 1)
     rows_a = ra[:HALO].astype(F32).reshape(HALO * PACK, COLS)
     rows_b = rb[:HALO].astype(F32).reshape(HALO * PACK, COLS)
     west = jnp.where(first_core, rows_b, rows_a).astype(BF16)
     east = jnp.where(first_core, rows_a, rows_b).astype(BF16)
-    window = jnp.concatenate([west, own_top[...].reshape(HALO * PACK, COLS), east], axis=1)
+    window = jnp.concatenate([west, own_top[:HALO].reshape(HALO * PACK, COLS), east], axis=1)
     src = iota((3 * COLS, WIDE), 0) - COLS
     t = iota((3 * COLS, WIDE), 1)
     q = t & 7
@@ -112,15 +131,15 @@
 
 
 def sigmoid(x):
-    return 1.0 / (1.0 + jnp.exp(-x))
+    return 0.5 * jnp.tanh(0.5 * x) + 0.5
 
 
 def main_kernel(
-    scal, spin, valid, own, grad, ce, rla, rlb, rf1, rf2, w1, wm, wmt, wl, wb, hi, lo,
+    scal, spin, valid, own, grad, ce, rla, rlb, w1, wm, wmt, wl, wb, hi, lo,
     state_out, closure_out, active_out,
     z0, z1, kxe, kxn, pres, gx, x3, g3, ybuf, acc_first, acc_rest, picked,
 ):
-    even, top = scal[2] == 1, scal[3] == 1
+    even = scal[2] == 1
 
     def place(y, left, corner_pack, slot):
         shift = (COLS - 8 * slot) % COLS
@@ -134,8 +153,7 @@
         return jnp.where(even, rlb[k].astype(F32), rla[k].astype(F32))
 
     def north(k):
-        near = jnp.where(even, rla[k].astype(F32), rlb[k].astype(F32))
-        return jnp.where(top, rf1[k].astype(F32) + rf2[k].astype(F32), near)
+        return jnp.where(even, rla[k].astype(F32), rlb[k].astype(F32))
 
     south_edge, north_edge, own_edge = south(HALO), north(HALO), ce[...].astype(F32)
     for k in range(HALO):
@@ -194,7 +212,7 @@
         step(z0, z1, i)
         return 0
 
-    lax.fori_loop(1, EXT - 1, first_step, 0, unroll=2)
+    lax.fori_loop(1, EXT - 1, first_step, 0, unroll=11)
 
     def second_pressure(y, _):
         pres[y] = pressure_scale * depth_sum(z1[y, T])
@@ -214,7 +232,7 @@
         g3[pl.ds(pl.multiple_of(PACK * y, 16), PACK), :] = tap_g.astype(BF16)
         return 0
 
-    lax.fori_loop(2, EXT - 2, second_step, 0, unroll=2)
+    lax.fori_loop(2, EXT - 2, second_step, 0, unroll=5)
     new = z0[HALO : HALO + ROWS, :INS, :COLS]
     for f in range(3):
         state_out[f] = jnp.swapaxes(new[:, LEV * f : LEV * (f + 1), :], 0, 1)
@@ -253,7 +271,7 @@
         )
         return 0
 
-    lax.fori_loop(0, ROWS, both_ways, 0)
+    lax.fori_loop(0, ROWS, both_ways, 0, unroll=4)
 
     closed = []
     for r in range(ROWS):
@@ -283,7 +301,7 @@
         picked[pl.ds(2 * c + 1, 1), :] = value[:, COLS:]
         return 0
 
-    lax.fori_loop(0, hi.shape[0] // 2, choose, 0, unroll=2)
+    lax.fori_loop(0, hi.shape[0] // 2, choose, 0, unroll=8)
     active_out[...] = picked[...].astype(BF16)
 
 
@@ -307,10 +325,10 @@
     return list(out.values())
 
 
-def reduce_over(x, axis, groups):
+def reduce_over(x, groups):
     count = len(groups[0])
     y = jnp.broadcast_to(x.astype(BF16)[None], (count,) + x.shape)
-    y = lax.all_to_all(y, axis, 0, 0, axis_index_groups=groups)
+    y = lax.all_to_all(y, BOTH, 0, 0, axis_index_groups=groups)
     return jnp.sum(y.astype(F32), axis=0)
 
 
@@ -329,6 +347,37 @@
     return hi.reshape(-1, COLS), lo.reshape(-1, COLS)
 
 
+def run_main(*args):
+    shape = jax.ShapeDtypeStruct
+    lines = args[-1].shape[0]
+    return pl.pallas_call(
+        main_kernel,
+        out_shape=(
+            shape((3, LEV, ROWS, COLS), F32),
+            shape((OUTS, ROWS, COLS), BF16),
+            shape((lines, COLS), BF16),
+        ),
+        in_specs=[smem()] * 3 + vmem(12),
+        out_specs=tuple(vmem(3)),
+        scratch_shapes=[
+            pltpu.VMEM((EXT, 4 * LEV, WIDE), F32),
+            pltpu.VMEM((EXT, 4 * LEV, WIDE), F32),
+            pltpu.VMEM((EXT, LEV, WIDE), F32),
+            pltpu.VMEM((EXT, LEV, WIDE), F32),
+            pltpu.VMEM((EXT, LEV, WIDE), F32),
+            pltpu.VMEM((EXT, OUTS, WIDE), F32),
+            pltpu.VMEM((EXT * TAPK, WIDE), BF16),
+            pltpu.VMEM((EXT * PACK, COLS), BF16),
+            pltpu.VMEM((EXT, 9 * OUTS, WIDE), F32),
+            pltpu.VMEM((CH, WIDE), F32),
+            pltpu.VMEM((CH, WIDE), F32),
+            pltpu.VMEM((lines, COLS), F32),
+        ],
+        compiler_params=params(),
+        name="main",
+    )(*args)
+
+
 def on_device(
     lon_count, lat_count,
     ocean_state, diffusivity, depth_levels, fold_pair, first_weight, mix_weight, last_weight, cotangent, active_index,
@@ -336,24 +385,27 @@
     lat, lon = lax.axis_index("lat"), lax.axis_index("lon")
     row_total, col_total = ROWS * lat_count, COLS * lon_count
     shape = jax.ShapeDtypeStruct
-    own, grad, top, bottom, edges = pl.pallas_call(
+    block = shape((HALO + 1, PACK, COLS), BF16)
+    own, grad, send, bottom = pl.pallas_call(
         functools.partial(prep_kernel, 1.0 / math.sqrt(row_total * col_total)),
         out_shape=(
             shape((ROWS, 4 * LEV, COLS), F32),
             shape((ROWS, OUTS, COLS), BF16),
+            block,
             shape((HALO, PACK, COLS), BF16),
-            shape((HALO, PACK, COLS), BF16),
-            shape((PACK, COLS), BF16),
         ),
-        in_specs=vmem(4),
-        out_specs=tuple(vmem(5)),
+        in_specs=[pl.BlockSpec(memory_space=pltpu.HBM)] * 4,
+        out_specs=tuple(vmem(4)),
+        scratch_shapes=[
+            pltpu.VMEM(x.shape, x.dtype) for x in (ocean_state, diffusivity, depth_levels, cotangent)
+        ]
+        + [pltpu.SemaphoreType.DMA((4,))],
         compiler_params=params(),
         name="prep",
     )(ocean_state, diffusivity, depth_levels, cotangent)
 
-    send = jnp.concatenate([top, edges[None]], axis=0)
+    rb = lax.ppermute(send, "lon", swap_pairs(lon_count, 1))
     ra = lax.ppermute(send, "lon", swap_pairs(lon_count, 0))
-    rb = lax.ppermute(send, "lon", swap_pairs(lon_count, 1) )
 
     folded = (fold_pair[0] - 3) % col_total
     turn, rel = folded // WIDE, folded % WIDE + 3
@@ -374,68 +426,52 @@
     wb = last_weight.reshape(3, 3, OUTS, CH)[::-1].reshape(9 * OUTS, CH).T
     wmt = mix_weight.T
 
-    block = shape((HALO + 1, PACK, COLS), BF16)
-    pla, plb, f1, f2, ce = pl.pallas_call(
+    pla, plb, plc, ce = pl.pallas_call(
         mid_kernel,
-        out_shape=(block, block, block, block, shape((PACK, COLS), BF16)),
+        out_shape=(block, block, block, shape((PACK, COLS), BF16)),
         in_specs=[smem()] + vmem(4),
-        out_specs=tuple(vmem(5)),
+        out_specs=tuple(vmem(4)),
         compiler_params=params(),
         name="mid",
-    )(scal, top, bottom, ra, rb)
-
-    near_a = swap_pairs(lat_count, 0)
-    near_b = swap_pairs(lat_count - 1, 1)
+    )(scal, send, bottom, rb, ra)
+
+    near_a = [(i * lat_count + a, i * lat_count + b) for i in range(lon_count) for a, b in swap_pairs(lat_count, 0)]
+    near_b = [
+        (i * lat_count + a, i * lat_count + b) for i in range(lon_count) for a, b in swap_pairs(lat_count - 1, 1)
+    ]
+    turns = lon_count // 2
 
     def exchange(q, second):
-        def run(pla, plb, f1, f2):
-            rf1 = lax.ppermute(f1, BOTH, fold_pairs(lon_count, lat_count, q))
+        def run(pla, plb, plc):
+            rlb = lax.ppermute(plb, BOTH, near_b + fold_pairs(lon_count, lat_count, q))
             if second:
-                rf2 = lax.ppermute(f2, BOTH, fold_pairs(lon_count, lat_count, q + 1))
-            else:
-                rf2 = jnp.zeros_like(f2)
-            return lax.ppermute(pla, "lat", near_a), lax.ppermute(plb, "lat", near_b), rf1, rf2
+                rlb = rlb + lax.ppermute(plc, BOTH, near_b + fold_pairs(lon_count, lat_count, (q + 1) % turns))
+            return rlb, lax.ppermute(pla, BOTH, near_a)
 
         return run
 
-    turns = lon_count // 2
     branches = [exchange(q, second) for q in range(turns) for second in (False, True)]
-    rla, rlb, rf1, rf2 = lax.switch(2 * turn + twice, branches, pla, plb, f1, f2)
-
-    lines = active_index.shape[0] // COLS
-    new_state, closure, active = pl.pallas_call(
-        main_kernel,
-        out_shape=(
-            shape((3, LEV, ROWS, COLS), F32),
-            shape((OUTS, ROWS, COLS), BF16),
-            shape((lines, COLS), BF16),
-        ),
-        in_specs=[smem()] * 3 + vmem(14),
-        out_specs=tuple(vmem(3)),
-        scratch_shapes=[
-            pltpu.VMEM((EXT, 4 * LEV, WIDE), F32),
-            pltpu.VMEM((EXT, 4 * LEV, WIDE), F32),
-            pltpu.VMEM((EXT, LEV, WIDE), F32),
-            pltpu.VMEM((EXT, LEV, WIDE), F32),
-            pltpu.VMEM((EXT, LEV, WIDE), F32),
-            pltpu.VMEM((EXT, OUTS, WIDE), F32),
-            pltpu.VMEM((EXT * TAPK, WIDE), BF16),
-            pltpu.VMEM((EXT * PACK, COLS), BF16),
-            pltpu.VMEM((EXT, 9 * OUTS, WIDE), F32),
-            pltpu.VMEM((CH, WIDE), F32),
-            pltpu.VMEM((CH, WIDE), F32),
-            pltpu.VMEM((lines, COLS), F32),
-        ],
-        compiler_params=params(),
-        name="main",
-    )(scal, spin, valid, own, grad, ce, rla, rlb, rf1, rf2, w1, mix_weight, wmt, wl, wb, hi, lo)
-
-    total = reduce_over(active, "lat", groups_of(lat_count, lambda i: 0))
-    total = reduce_over(total, "lon", groups_of(lon_count, lambda i: i // 16))
-    mine = total.astype(BF16)
-    half = lon_count // 2
-    other = lax.ppermute(mine, "lon", [(i, (i + half) % lon_count) for i in range(lon_count)])
-    total = mine.astype(F32) + other.astype(F32)
+    rlb, rla = lax.switch(2 * turn + twice, branches, pla, plb, plc)
+
+    new_state, closure, active = run_main(
+        scal, spin, valid, own, grad, ce, rla, rlb, w1, mix_weight, wmt, wl, wb, hi, lo
+    )
+
+    halves, cores, quads = 2, 2, 4
+    inner = lon_count // halves
+    everyone = lon_count * lat_count
+
+    def place_of(d):
+        lon_at, lat_at = divmod(d, lat_count)
+        z_hi, low = divmod(lon_at, inner)
+        return z_hi, low // cores, low % cores, lat_at // quads, lat_at % quads
+
+    def grouped(kept):
+        return groups_of(everyone, lambda d: tuple(place_of(d)[i] for i in kept))
+
+    total = reduce_over(active, grouped((0, 1, 3)))
+    total = reduce_over(total, grouped((0, 2, 3, 4)))
+    total = reduce_over(total, grouped((1, 2, 4)))
     return new_state, closure, total.reshape(-1)
 
 

time: 103 us -> 87.2 us (0.85); the launches traced: 102 us -> 85.5 us
  blocking collectives: 46.2 us -> 34.6 us
  Pallas kernels: 21.2 us -> 16.3 us
    all_to_all x2 -> x3, blocking collectives: 46.2 us -> 34.6 us  [reduce_over(): y = lax.all_to_all(y, BOTH, 0, 0, axis_index_groups=groups)]
    ppermute x4 -> x2, starting transfers between devices: 12.5 us -> 6.25 us  [the longest x1 4.96 us: run(): return (rlb, lax.ppermute(pla, BOTH, near_a))]
    pallas_call x2, Pallas kernels: 21 us -> 15.7 us  [the longest x1 15.1 us: run_main(): pl.pallas_call(main_kernel, out_shape=(shape((3, LEV, ROWS, COLS), F32),...]
    ppermute x1, starting transfers between devices: 8.79 us -> 12.1 us  [on_device(): ra = lax.ppermute(send, 'lon', swap_pairs(lon_count, 0))]
    ppermute x1, starting transfers between devices: 1.92 us -> 4.59 us  [on_device(): rb = lax.ppermute(send, 'lon', swap_pairs(lon_count, 1))]
    ppermute x4 -> x2, waiting for transfers between devices: 1.73 us -> 2.25 us  [the longest x1 2.24 us: run(): return (rlb, lax.ppermute(pla, BOTH, near_a))]
  transfers between devices with their start and end apart: 6 -> 4, of which waited for: 2 -> 1; matrix products, arithmetic and copies ran while one was open for 2% -> 2% of each run, Pallas kernels for 0% -> 0%
where the time goes in v2:
time: 87.2 us; the launch traced here: 85.5 us
  blocking collectives  34.6 us (40%)
  starting transfers between devices  22.9 us (26%)
  Pallas kernels  16.3 us (19%)
  local copies, waits for them, and re-layouts  6.75 us (8%)
  waiting for transfers between devices  2.25 us (3%)
  between operations  1.53 us (2%)
  other arithmetic  1.05 us (1%)
    all_to_all x3, blocking collectives, reduce_over(): y = lax.all_to_all(y, BOTH, 0, 0, axis_index_groups=groups)  34.6 us
    pallas_call x1, Pallas kernels, run_main(): pl.pallas_call(main_kernel, out_shape=(shape((3, LEV, ROWS, COLS), F32),...  15.1 us
    ppermute x1, starting transfers between devices, on_device(): ra = lax.ppermute(send, 'lon', swap_pairs(lon_count, 0))  12.1 us
    unnamed x17, local copies, waits for them, and re-layouts  5.3 us
    ppermute x1, starting transfers between devices, run(): return (rlb, lax.ppermute(pla, BOTH, near_a))  4.96 us
    ppermute x1, starting transfers between devices, on_device(): rb = lax.ppermute(send, 'lon', swap_pairs(lon_count, 1))  4.59 us
    ppermute x1, waiting for transfers between devices, run(): return (rlb, lax.ppermute(pla, BOTH, near_a))  2.24 us
  transfers between devices with their start and end apart: 4, of which 1 were waited for; matrix products, arithmetic and copies ran while one was open for 2% of the time, Pallas kernels for 0%

profile of v2, /device:TPU:1, one launch (start us, length us, event | category | flops | bytes accessed | tf_op | source)
XLA Modules:
  0.0 85.5 jit_solution(5167853644890980207)
XLA Ops:
  0.6 0.0 copy-start
  0.6 0.9 %copy-done = f32[3,8,16,128]{3,2,1,0:T(8,128)S(1)} copy-done((f32[3,8,16,128]{3,2,1,0:T(8,128)S(1)}, f32[3,8,16,128]{3,2,1,0:T(8,128)}, u32[]{:S(2)}) %copy-start) | copy-done | bytes 196632
  1.6 0.0 copy-start.3
  1.6 0.8 copy-done.3
  2.4 0.0 copy-start.4
  2.4 0.8 copy-done.4
  3.2 0.0 copy-start.5
  3.2 0.7 copy-done.5
  3.9 0.6 prep.1
  4.6 4.6 %collective-permute-start.80 = (bf16[5,48,128]{2,1,0:T(8,128)(2,1)S(1)}, bf16[5,48,128]{2,1,0:T(8,128)(2,1)S(1)}, u32[]{:S(2)}, u32[]{:S(2)}) collective-permute-start(bf16[5,48,128]{2,1,0:T(8,128)(2,1)S(1)} %get-tuple-element.258.own_top), channel_id=1, source_target_pairs={{16,32},{32,16},{48,64},{64,48},{80,96},{96,80},{112,128},{128,112... | collective-permute-start | bytes 184328 | tf_op jit(solution)/shard_map/ppermute | solution.py:407
  9.2 12.1 %collective-permute-start.81 = (bf16[5,48,128]{2,1,0:T(8,128)(2,1)S(1)}, bf16[5,48,128]{2,1,0:T(8,128)(2,1)S(1)}, u32[]{:S(2)}, u32[]{:S(2)}) collective-permute-start(bf16[5,48,128]{2,1,0:T(8,128)(2,1)S(1)} %get-tuple-element.258.own_top), channel_id=1, source_target_pairs={{0,16},{16,0},{32,48},{48,32},{64,80},{80,64},{96,112},{112,96},{1... | collective-permute-start | bytes 184328 | tf_op jit(solution)/shard_map/ppermute | solution.py:408
  21.3 1.2 %slice.3 = s32[1]{0:T(128)} slice(s32[4096]{0:T(1024)} %param.44), slice={[0:1]} | slice | bytes 8 | tf_op jit(solution)/shard_map/slice | solution.py:410
  23.1 0.0 copy-start.7
  23.3 0.0 copy-start.6
  23.3 0.6 copy-done.7
  23.9 0.2 fusion.14
  24.1 0.0 copy-done.6
  24.2 0.0 copy-start.1
  24.2 0.1 copy.21.w1
  24.3 0.7 copy-done.1
  24.9 0.0 copy-start.2
  25.0 0.1 copy.20
  25.0 0.6 copy-done.2
  25.7 0.1 copy.19
  25.8 0.1 pad_add_fusion.scal
  25.9 0.0 collective-permute-done.80.rb
  25.9 0.0 collective-permute-done.81.ra
  25.9 0.6 mid.1
  26.4 8.6 %conditional.1 = (bf16[5,48,128]{2,1,0:T(8,128)(2,1)}, bf16[5,48,128]{2,1,0:T(8,128)(2,1)}) conditional(s32[]{:T(128)} %clamp.3, (bf16[5,48,128]{2,1,0:T(8,128)(2,1)S(1)}, bf16[5,48,128]{2,1,0:T(8,128)(2,1)S(1)}) %tuple.136, (bf16[5,48,128]{2,1,0:T(8,128)(2,1)S(1)}, bf16[5,48,128]{2,1,0:T(8,128)(2,1)S(1)}, ...), branch_computations={%region_0.1_spmd, %region_1.2_spmd, %region_2.3_spmd, %region_3.4_... | conditional | flops 30720 | bytes 921736 | solution.py:454
  26.5 1.3 %collective-permute-start.45 = (bf16[5,48,128]{2,1,0:T(8,128)(2,1)S(1)}, bf16[5,48,128]{2,1,0:T(8,128)(2,1)}, u32[]{:S(2)}, u32[]{:S(2)}) collective-permute-start(bf16[5,48,128]{2,1,0:T(8,128)(2,1)S(1)} %get-tuple-element.205), channel_id=1, source_target_pairs={{1,2},{2,1},{3,4},{4,3},{5,6},{6,5},{7,8},{8,7},{9,10},{10,9},{11,... | collective-permute-start | bytes 184328 | tf_op jit(solution)/shard_map/cond/branch_18_fun/ppermute | solution.py:446
  27.8 5.0 %collective-permute-start.46 = (bf16[5,48,128]{2,1,0:T(8,128)(2,1)S(1)}, bf16[5,48,128]{2,1,0:T(8,128)(2,1)}, u32[]{:S(2)}, u32[]{:S(2)}) collective-permute-start(bf16[5,48,128]{2,1,0:T(8,128)(2,1)S(1)} %get-tuple-element.206), channel_id=1, source_target_pairs={{0,1},{1,0},{2,3},{3,2},{4,5},{5,4},{6,7},{7,6},{8,9},{9,8},{10,11... | collective-permute-start | bytes 184328 | tf_op jit(solution)/shard_map/cond/branch_18_fun/ppermute | solution.py:449
  32.8 0.0 collective-permute-done.45
  32.8 2.2 %collective-permute-done.46 = bf16[5,48,128]{2,1,0:T(8,128)(2,1)} collective-permute-done((bf16[5,48,128]{2,1,0:T(8,128)(2,1)S(1)}, bf16[5,48,128]{2,1,0:T(8,128)(2,1)}, u32[]{:S(2)}, u32[]{:S(2)}) %collective-permute-start.46) | collective-permute-done | bytes 61472 | tf_op jit(solution)/shard_map/cond/branch_18_fun/ppermute | solution.py:449
  35.0 15.1 %main.1 = (f32[3,8,16,128]{3,2,1,0:T(8,128)}, bf16[16,16,128]{2,1,0:T(8,128)(2,1)}, bf16[64,128]{1,0:T(8,128)(2,1)S(1)}) custom-call(s32[4]{0:T(128)S(1)} %pad_add_fusion.scal, f32[24]{0:T(128)S(1)} %fusion.31.spin, f32[24]{0:T(128)S(1)} %and_convert_fusion.valid, f32[16,32,128]{2,1,0:T(8,128)S(1)} %get-tuple-element.256.own, ...), custom_call_target="tpu_custom_call" | custom-call | tf_op jit(solution)/shard_map/main/pallas_call | solution.py:353
  50.1 10.0 %all_to_all.15 = bf16[8,64,128]{2,1,0:T(8,128)(2,1)S(1)} all-to-all(bf16[8,64,128]{2,1,0:T(8,128)(2,1)S(1)} %broadcast_in_dim.6), channel_id=1, replica_groups={{0,1,2,3,16,17,18,19},{4,5,6,7,20,21,22,23},{8,9,10,11,24,25,26,27},{12..., dimensions={0} | all-to-all | bytes 262144 | tf_op jit(solution)/shard_map/all_to_all | solution.py:331
  60.2 10.8 %all_to_all.16 = bf16[8,64,128]{2,1,0:T(8,128)(2,1)S(1)} all-to-all(bf16[8,64,128]{2,1,0:T(8,128)(2,1)S(1)} %broadcast_in_dim.7), channel_id=1, replica_groups={{0,32,64,96,128,160,192,224},{1,33,65,97,129,161,193,225},{2,34,66,98,1..., dimensions={0} | all-to-all | bytes 262144 | tf_op jit(solution)/shard_map/all_to_all | solution.py:331
  71.0 13.8 %all_to_all.17 = bf16[8,64,128]{2,1,0:T(8,128)(2,1)S(1)} all-to-all(bf16[8,64,128]{2,1,0:T(8,128)(2,1)S(1)} %broadcast_in_dim.8), channel_id=1, replica_groups={{0,4,8,12,256,260,264,268},{1,5,9,13,257,261,265,269},{2,6,10,14,258,26..., dimensions={0} | all-to-all | bytes 262144 | tf_op jit(solution)/shard_map/all_to_all | solution.py:331
  84.8 0.6 convert_reduce_fusion
  (9 shorter events, 0.2 us)
Async XLA Ops:
  0.6 0.9 %copy-start = (f32[3,8,16,128]{3,2,1,0:T(8,128)S(1)}, f32[3,8,16,128]{3,2,1,0:T(8,128)}, u32[]{:S(2)}) copy-start(f32[3,8,16,128]{3,2,1,0:T(8,128)} %state_hbm.1) | copy-start | bytes 589828
  1.6 0.8 copy-start.3
  2.4 0.8 copy-start.4
  3.2 0.7 copy-start.5
  4.6 21.3 %collective-permute-start.80 = (bf16[5,48,128]{2,1,0:T(8,128)(2,1)S(1)}, bf16[5,48,128]{2,1,0:T(8,128)(2,1)S(1)}, u32[]{:S(2)}, u32[]{:S(2)}) collective-permute-start(bf16[5,48,128]{2,1,0:T(8,128)(2,1)S(1)} %get-tuple-element.258.own_top), channel_id=1, source_target_pairs={{16,32},{32,16},{48,64},{64,48},{80,96},{96,80},{112,128},{128,112... | collective-permute-start | bytes 184328 | tf_op jit(solution)/shard_map/ppermute | solution.py:407
  9.2 16.7 %collective-permute-start.81 = (bf16[5,48,128]{2,1,0:T(8,128)(2,1)S(1)}, bf16[5,48,128]{2,1,0:T(8,128)(2,1)S(1)}, u32[]{:S(2)}, u32[]{:S(2)}) collective-permute-start(bf16[5,48,128]{2,1,0:T(8,128)(2,1)S(1)} %get-tuple-element.258.own_top), channel_id=1, source_target_pairs={{0,16},{16,0},{32,48},{48,32},{64,80},{80,64},{96,112},{112,96},{1... | collective-permute-start | bytes 184328 | tf_op jit(solution)/shard_map/ppermute | solution.py:408
  23.1 0.8 copy-start.7
  23.3 0.9 %copy-start.6 = (bf16[9,64,24]{1,2,0:T(8,128)(2,1)S(1)}, bf16[9,64,24]{1,2,0:T(8,128)(2,1)}, u32[]{:S(2)}) copy-start(bf16[9,64,24]{1,2,0:T(8,128)(2,1)} %param.45) | copy-start | bytes 82948
  24.2 0.8 copy-start.1
  24.9 0.7 copy-start.2
  26.5 6.3 %collective-permute-start.45 = (bf16[5,48,128]{2,1,0:T(8,128)(2,1)S(1)}, bf16[5,48,128]{2,1,0:T(8,128)(2,1)}, u32[]{:S(2)}, u32[]{:S(2)}) collective-permute-start(bf16[5,48,128]{2,1,0:T(8,128)(2,1)S(1)} %get-tuple-element.205), channel_id=1, source_target_pairs={{1,2},{2,1},{3,4},{4,3},{5,6},{6,5},{7,8},{8,7},{9,10},{10,9},{11,... | collective-permute-start | bytes 184328 | tf_op jit(solution)/shard_map/cond/branch_18_fun/ppermute | solution.py:446
  27.8 7.2 %collective-permute-start.46 = (bf16[5,48,128]{2,1,0:T(8,128)(2,1)S(1)}, bf16[5,48,128]{2,1,0:T(8,128)(2,1)}, u32[]{:S(2)}, u32[]{:S(2)}) collective-permute-start(bf16[5,48,128]{2,1,0:T(8,128)(2,1)S(1)} %get-tuple-element.206), channel_id=1, source_target_pairs={{0,1},{1,0},{2,3},{3,2},{4,5},{5,4},{6,7},{7,6},{8,9},{9,8},{10,11... | collective-permute-start | bytes 184328 | tf_op jit(solution)/shard_map/cond/branch_18_fun/ppermute | solution.py:449

commit v3 on v2

--- a/solution.py
+++ b/solution.py
@@ -26,6 +26,8 @@
 TAPK = 80
 FIRST = 9 * CH * INS
 MIX = CH * CH
+GRANT = 60
+SHARE = 8
 BOTH = ("lon", "lat")
 F32 = jnp.float32
 BF16 = jnp.bfloat16
@@ -48,14 +50,23 @@
 
 
 def prep_kernel(
-    grad_scale, state_hbm, kappa_hbm, depth_hbm, cot_hbm, own, grad, send, bottom, state, kappa, depth, cot, sems
+    grad_scale, col_total, lat_count, state_hbm, kappa_hbm, depth_hbm, cot_hbm, fold_hbm,
+    own, grad, send, bottom, scal, turn, state, kappa, depth, cot, fold, sems,
 ):
-    pairs = ((state_hbm, state), (kappa_hbm, kappa), (depth_hbm, depth), (cot_hbm, cot))
+    lat, lon = lax.axis_index("lat"), lax.axis_index("lon")
+    pairs = ((state_hbm, state), (kappa_hbm, kappa), (depth_hbm, depth), (cot_hbm, cot), (fold_hbm, fold))
     copies = [pltpu.make_async_copy(a, b, sems.at[i]) for i, (a, b) in enumerate(pairs)]
     for copy in copies:
         copy.start()
     for copy in copies:
         copy.wait()
+    folded = lax.rem(fold[0] + col_total - 3, col_total)
+    rel = lax.rem(folded, WIDE) + 3
+    scal[0] = lax.rem(lon, 2)
+    scal[1] = rel
+    scal[2] = (lax.rem(lat, 2) == 0).astype(jnp.int32)
+    scal[3] = (lat == lat_count - 1).astype(jnp.int32)
+    turn[0] = 2 * lax.div(folded, WIDE) + (rel + 4 >= WIDE).astype(jnp.int32)
     level = iota((LEV, COLS), 0)
     lane = iota((PACK, COLS), 1)
     fields = [jnp.swapaxes(state[f], 0, 1) for f in range(3)]
@@ -79,7 +90,7 @@
     send[HALO] = packed.astype(BF16)
 
 
-def mid_kernel(scal, own_top, own_bottom, rb, ra, pla, plb, plc, corner):
+def mid_kernel(scal, own_top, own_bottom, ra, rb, pla, plb, plc, corner):
     core, rel, even, at_top = scal[0], scal[1], scal[2], scal[3] == 1
     lane = iota((PACK, COLS), 1)
     first_core = core == 0
@@ -134,12 +145,46 @@
     return 0.5 * jnp.tanh(0.5 * x) + 0.5
 
 
+def placed_entries(active_index):
+    def split(x, by):
+        whole = lax.div(x, jnp.full_like(x, by))
+        return whole, x - whole * by
+
+    n = active_index
+    k, rem = split(n, CH * INS)
+    (dy, dx), (o, c) = split(k, 3), split(rem, INS)
+    hi_a, lo_a = dy * TAPK + dx * INS + c, o
+    o, c = split(n - FIRST, CH)
+    hi_b, lo_b = 9 * OUTS + c, CH + o
+    k, rem = split(n - FIRST - MIX, OUTS * CH)
+    (dy, dx), (o, c) = split(k, 3), split(rem, CH)
+    hi_c, lo_c = (2 - dy) * PACK + dx * OUTS + o, CH + c
+    in_a, in_b = n < FIRST, n < FIRST + MIX
+    hi = jnp.where(in_a, hi_a, jnp.where(in_b, hi_b, hi_c))
+    lo = jnp.where(in_a, lo_a, jnp.where(in_b, lo_b, lo_c))
+    return hi, lo
+
+
 def main_kernel(
-    scal, spin, valid, own, grad, ce, rla, rlb, w1, wm, wmt, wl, wb, hi, lo,
+    row_total, own, grad, ce, rla, rlb, first_hbm, mix_hbm, last_hbm, entries_hbm,
     state_out, closure_out, active_out,
     z0, z1, kxe, kxn, pres, gx, x3, g3, ybuf, acc_first, acc_rest, picked,
+    first_taps, mix, last, entries, w1, wmt, wl, wb, hi, lo, spin, sems,
 ):
-    even = scal[2] == 1
+    pairs = ((first_hbm, first_taps), (mix_hbm, mix), (last_hbm, last), (entries_hbm, entries))
+    copies = [pltpu.make_async_copy(a, b, sems.at[i]) for i, (a, b) in enumerate(pairs)]
+    for copy in copies:
+        copy.start()
+    lat = lax.axis_index("lat")
+    even = lax.rem(lat, 2) == 0
+    first_row = lat * ROWS - HALO
+    at_row = first_row + iota((EXT, COLS), 0)
+    mirrored = jnp.where(at_row >= row_total, 2 * row_total - 1 - at_row, at_row)
+    spin[...] = coriolis_peak * jnp.sin(math.pi * (mirrored.astype(F32) + 0.5) / row_total - 0.5 * math.pi)
+
+    def valid(y):
+        return jnp.where((first_row + y >= 0) & (first_row + y < row_total), 1.0, 0.0)
+
 
     def place(y, left, corner_pack, slot):
         shift = (COLS - 8 * slot) % COLS
@@ -191,7 +236,8 @@
         ke, kn, ks = kxe[y], kxn[y], kxn[y - 1]
         u, v, t = src[y, U], src[y, V], src[y, T]
         wet = (z0[y, K] > 0).astype(F32)
-        f = spin[y]
+        row = spin[pl.ds(y, 1), :]
+        f = jnp.concatenate([row, row], axis=1)
 
         def diffuse(z, zn, zs):
             flux = ke * (east(z) - z)
@@ -220,12 +266,12 @@
 
     lax.fori_loop(1, EXT - 1, second_pressure, 0, unroll=2)
 
-    zero_rows = jnp.zeros((TAPK - 3 * INS, WIDE), F32)
+    zero_rows = jnp.zeros((TAPK - 3 * INS, COLS), F32)
 
     def second_step(y, _):
         step(z1, z0, y)
-        x = z0[y, :INS] * valid[y]
-        taps = jnp.concatenate([west(x), x, east(x), zero_rows], axis=0)
+        x = z0[y, :INS] * valid(y)
+        taps = jnp.concatenate([west(x)[:, :COLS], x[:, :COLS], east(x)[:, :COLS], zero_rows], axis=0)
         x3[pl.ds(pl.multiple_of(TAPK * y, 16), TAPK), :] = taps.astype(BF16)
         g = gx[y]
         tap_g = jnp.concatenate([east(g), g, west(g)], axis=0)[:, :COLS]
@@ -237,43 +283,88 @@
     for f in range(3):
         state_out[f] = jnp.swapaxes(new[:, LEV * f : LEV * (f + 1), :], 0, 1)
 
-    def forward(y):
-        taps = x3[pl.ds(pl.multiple_of(TAPK * (y - 1), 16), 3 * TAPK), :]
+    for copy in copies:
+        copy.wait()
+    pieces = []
+    for k in range(9):
+        pieces.append(first_taps[k].astype(F32))
+        if k % 3 == 2:
+            pieces.append(jnp.zeros((TAPK - 3 * INS, CH), F32))
+    w1[...] = jnp.concatenate(pieces, axis=0).T.astype(BF16)
+    wmt[...] = mix[...].astype(F32).T.astype(BF16)
+    taps_of = [last[k].astype(F32) for k in range(9)]
+    wl[...] = jnp.concatenate(taps_of, axis=0).astype(BF16)
+    wb[...] = jnp.concatenate(taps_of[6:] + taps_of[3:6] + taps_of[:3], axis=0).T.astype(BF16)
+    hi[...], lo[...] = placed_entries(entries[...])
+
+    def hidden(taps):
         pre1 = jnp.dot(w1[...], taps, preferred_element_type=F32)
         s1 = sigmoid(pre1)
         h1 = (pre1 * s1).astype(BF16)
-        pre2 = jnp.dot(wm[...], h1, preferred_element_type=F32)
+        pre2 = jnp.dot(mix[...], h1, preferred_element_type=F32)
         s2 = sigmoid(pre2)
-        h2 = (pre2 * s2 * valid[y]).astype(BF16)
-        ybuf[y] = jnp.dot(wl[...], h2, preferred_element_type=F32)
-        return taps, pre1, s1, h1, pre2, s2, h2
-
-    forward(HALO - 1)
-    forward(HALO + ROWS)
+        return pre1, s1, h1, pre2, s2, pre2 * s2
+
+    def two_rows(ref, depth, y, z):
+        return jnp.concatenate(
+            [ref[pl.ds(pl.multiple_of(depth * (r - 1), 16), 3 * depth), :] for r in (y, z)], axis=1
+        )
+
+    def spread(h2):
+        return jnp.dot(wl[...], h2.astype(BF16), preferred_element_type=F32)
+
+    lane = iota((INS, COLS), 1)
+    columns = [jnp.zeros((INS, COLS), F32)] * 3
+    for y in range(2, EXT - 2):
+        x = z0[y, :INS] * valid(y)
+        inner, outer = x[:, :COLS], x[:, COLS:]
+        sides = (jnp.where(lane == COLS - 1, inner, outer), outer, jnp.where(lane == 0, inner, outer))
+        for d in range(3):
+            moved = pltpu.roll(sides[d], 2 * y + 2 - d, 1)
+            columns[d] = jnp.where((lane >> 1) == y, moved, columns[d])
+    side_taps = []
+    for shift in (2, 0, COLS - 2):
+        side_taps += [pltpu.roll(c, shift, 1) if shift else c for c in columns] + [zero_rows]
+    side_row = first_row + (iota((CH, COLS), 1) >> 1)
+    side_valid = ((side_row >= 0) & (side_row < row_total)).astype(F32)
+    side = spread(hidden(jnp.concatenate(side_taps, axis=0).astype(BF16))[5] * side_valid)
+    side_sum = []
+    for d in (0, 2):
+        parts = [side[OUTS * (3 * k + d) : OUTS * (3 * k + d + 1)] for k in range(3)]
+        side_sum.append(pltpu.roll(parts[0], 2, 1) + parts[1] + pltpu.roll(parts[2], COLS - 2, 1))
+
+    low, high = HALO - 1, HALO + ROWS
+    h2 = hidden(two_rows(x3, TAPK, low, high))[5]
+    ends = spread(jnp.concatenate([h2[:, :COLS] * valid(low), h2[:, COLS:] * valid(high)], axis=1))
+    ybuf[low] = ends[:, :COLS]
+    ybuf[high] = ends[:, COLS:]
     acc_first[...] = jnp.zeros_like(acc_first)
     acc_rest[...] = jnp.zeros_like(acc_rest)
     nt = (((1,), (1,)), ((), ()))
 
     def both_ways(i, _):
-        y = HALO + i
-        taps, pre1, s1, h1, pre2, s2, h2 = (x[:, :COLS] for x in forward(y))
-        g9 = g3[pl.ds(pl.multiple_of(PACK * (y - 1), 16), 3 * PACK), :]
+        y = HALO + 2 * i
+        taps = two_rows(x3, TAPK, y, y + 1)
+        pre1, s1, h1, pre2, s2, act = hidden(taps)
+        h2 = act.astype(BF16)
+        out = spread(h2)
+        ybuf[y] = out[:, :COLS]
+        ybuf[y + 1] = out[:, COLS:]
+        g9 = two_rows(g3, PACK, y, y + 1)
         back2 = jnp.dot(wb[...], g9, preferred_element_type=F32)
         d2 = (back2 * (s2 * (1.0 + pre2 * (1.0 - s2)))).astype(BF16)
         back1 = jnp.dot(wmt[...], d2, preferred_element_type=F32)
         d1 = (back1 * (s1 * (1.0 + pre1 * (1.0 - s1)))).astype(BF16)
         acc_first[:, : 3 * TAPK] += lax.dot_general(d1, taps, nt, preferred_element_type=F32)
-        gap = jnp.zeros((16, COLS), BF16)
-        right = jnp.concatenate([jnp.zeros((160, COLS), BF16), h1, jnp.zeros((32, COLS), BF16)], axis=0)
-        left = jnp.concatenate([g9, gap, jnp.zeros((96, COLS), BF16)], axis=0)
-        acc_rest[...] += lax.dot_general(h2, left, nt, preferred_element_type=F32) + lax.dot_general(
-            d2, right, nt, preferred_element_type=F32
+        acc_rest[:, : 9 * OUTS + CH] += lax.dot_general(
+            jnp.concatenate([h2, d2], axis=0), jnp.concatenate([g9, h1], axis=0), nt, preferred_element_type=F32
         )
         return 0
 
-    lax.fori_loop(0, ROWS, both_ways, 0, unroll=4)
+    lax.fori_loop(0, ROWS // 2, both_ways, 0, unroll=8)
 
     closed = []
+    lane = iota((OUTS, COLS), 1)
     for r in range(ROWS):
         y = HALO + r
         part = [
@@ -282,12 +373,17 @@
             + ybuf[y + 1, OUTS * (6 + d) : OUTS * (7 + d)]
             for d in range(3)
         ]
-        total = (west(part[0]) + part[1] + east(part[2]))[:, :COLS]
+        from_west = jnp.where(lane == 0, pltpu.roll(side_sum[0], COLS - 2 * y, 1), pltpu.roll(part[0], 1, 1))
+        from_east = jnp.where(
+            lane == COLS - 1, pltpu.roll(side_sum[1], COLS - 2 - 2 * y, 1), pltpu.roll(part[2], COLS - 1, 1)
+        )
         wet = (own[r, K] > 0).astype(F32)
-        closed.append(jnp.concatenate([wet, wet], axis=0) * total)
+        closed.append(jnp.concatenate([wet, wet], axis=0) * (from_west + part[1] + from_east))
     closure_out[...] = jnp.swapaxes(jnp.stack(closed), 0, 1).astype(BF16)
 
-    table = jnp.concatenate([acc_first[...], acc_rest[...]], axis=0).astype(BF16)
+    is_last = iota((CH, WIDE), 1) < 9 * OUTS
+    rest = jnp.where(is_last, acc_rest[:CH], acc_rest[CH:])
+    table = jnp.concatenate([acc_first[...], rest], axis=0).astype(BF16)
     column = iota((WIDE, WIDE), 0)
     line = iota((2 * CH, WIDE), 0)
 
@@ -302,7 +398,9 @@
         return 0
 
     lax.fori_loop(0, hi.shape[0] // 2, choose, 0, unroll=8)
-    active_out[...] = picked[...].astype(BF16)
+    chosen = picked[...].astype(BF16)
+    for k in range(SHARE):
+        active_out[k] = chosen
 
 
 def swap_pairs(count, start):
@@ -325,39 +423,26 @@
     return list(out.values())
 
 
-def reduce_over(x, groups):
-    count = len(groups[0])
-    y = jnp.broadcast_to(x.astype(BF16)[None], (count,) + x.shape)
-    y = lax.all_to_all(y, BOTH, 0, 0, axis_index_groups=groups)
-    return jnp.sum(y.astype(F32), axis=0)
-
-
-def placed_entries(active_index):
-    n = active_index
-    k, rem = n // (CH * INS), n % (CH * INS)
-    hi_a, lo_a = (k // 3) * TAPK + (k % 3) * INS + rem % INS, rem // INS
-    g = n - FIRST
-    hi_b, lo_b = 160 + g % CH, CH + g // CH
-    g = n - FIRST - MIX
-    k, rem = g // (OUTS * CH), g % (OUTS * CH)
-    hi_c, lo_c = (2 - k // 3) * PACK + (k % 3) * OUTS + rem // CH, CH + rem % CH
-    in_a, in_b = n < FIRST, n < FIRST + MIX
-    hi = jnp.where(in_a, hi_a, jnp.where(in_b, hi_b, hi_c))
-    lo = jnp.where(in_a, lo_a, jnp.where(in_b, lo_b, lo_c))
-    return hi.reshape(-1, COLS), lo.reshape(-1, COLS)
-
-
-def run_main(*args):
+def reduce_over(shares, groups):
+    arrived = lax.all_to_all(shares, BOTH, 0, 0, axis_index_groups=groups)
+    return jnp.sum(arrived.astype(F32), axis=0)
+
+
+def shared(x):
+    return jnp.broadcast_to(x.astype(BF16)[None], (SHARE,) + x.shape)
+
+
+def run_main(row_total, *args):
     shape = jax.ShapeDtypeStruct
     lines = args[-1].shape[0]
     return pl.pallas_call(
-        main_kernel,
+        functools.partial(main_kernel, row_total),
         out_shape=(
             shape((3, LEV, ROWS, COLS), F32),
             shape((OUTS, ROWS, COLS), BF16),
-            shape((lines, COLS), BF16),
+            shape((SHARE, lines, COLS), BF16),
         ),
-        in_specs=[smem()] * 3 + vmem(12),
+        in_specs=vmem(5) + [pl.BlockSpec(memory_space=pltpu.HBM)] * 4,
         out_specs=tuple(vmem(3)),
         scratch_shapes=[
             pltpu.VMEM((EXT, 4 * LEV, WIDE), F32),
@@ -366,14 +451,25 @@
             pltpu.VMEM((EXT, LEV, WIDE), F32),
             pltpu.VMEM((EXT, LEV, WIDE), F32),
             pltpu.VMEM((EXT, OUTS, WIDE), F32),
-            pltpu.VMEM((EXT * TAPK, WIDE), BF16),
+            pltpu.VMEM((EXT * TAPK, COLS), BF16),
             pltpu.VMEM((EXT * PACK, COLS), BF16),
-            pltpu.VMEM((EXT, 9 * OUTS, WIDE), F32),
+            pltpu.VMEM((EXT, 9 * OUTS, COLS), F32),
             pltpu.VMEM((CH, WIDE), F32),
-            pltpu.VMEM((CH, WIDE), F32),
+            pltpu.VMEM((2 * CH, WIDE), F32),
             pltpu.VMEM((lines, COLS), F32),
+        ]
+        + [pltpu.VMEM(x.shape, x.dtype) for x in args[-4:]]
+        + [
+            pltpu.VMEM((CH, 3 * TAPK), BF16),
+            pltpu.VMEM((CH, CH), BF16),
+            pltpu.VMEM((9 * OUTS, CH), BF16),
+            pltpu.VMEM((CH, 9 * OUTS), BF16),
+            pltpu.VMEM((lines, COLS), jnp.int32),
+            pltpu.VMEM((lines, COLS), jnp.int32),
+            pltpu.VMEM((EXT, COLS), F32),
+            pltpu.SemaphoreType.DMA((4,)),
         ],
-        compiler_params=params(),
+        compiler_params=params(GRANT),
         name="main",
     )(*args)
 
@@ -386,54 +482,40 @@
     row_total, col_total = ROWS * lat_count, COLS * lon_count
     shape = jax.ShapeDtypeStruct
     block = shape((HALO + 1, PACK, COLS), BF16)
-    own, grad, send, bottom = pl.pallas_call(
-        functools.partial(prep_kernel, 1.0 / math.sqrt(row_total * col_total)),
+    own, grad, send, bottom, scal, turn = pl.pallas_call(
+        functools.partial(prep_kernel, 1.0 / math.sqrt(row_total * col_total), col_total, lat_count),
         out_shape=(
             shape((ROWS, 4 * LEV, COLS), F32),
             shape((ROWS, OUTS, COLS), BF16),
             block,
             shape((HALO, PACK, COLS), BF16),
+            shape((4,), jnp.int32),
+            shape((1,), jnp.int32),
         ),
-        in_specs=[pl.BlockSpec(memory_space=pltpu.HBM)] * 4,
-        out_specs=tuple(vmem(4)),
+        in_specs=[pl.BlockSpec(memory_space=pltpu.HBM)] * 5,
+        out_specs=tuple(vmem(4) + [smem()] * 2),
         scratch_shapes=[
             pltpu.VMEM(x.shape, x.dtype) for x in (ocean_state, diffusivity, depth_levels, cotangent)
         ]
-        + [pltpu.SemaphoreType.DMA((4,))],
-        compiler_params=params(),
+        + [pltpu.SMEM(fold_pair.shape, jnp.int32), pltpu.SemaphoreType.DMA((5,))],
+        compiler_params=params(GRANT),
         name="prep",
-    )(ocean_state, diffusivity, depth_levels, cotangent)
+    )(ocean_state, diffusivity, depth_levels, cotangent, fold_pair)
 
     rb = lax.ppermute(send, "lon", swap_pairs(lon_count, 1))
     ra = lax.ppermute(send, "lon", swap_pairs(lon_count, 0))
 
-    folded = (fold_pair[0] - 3) % col_total
-    turn, rel = folded // WIDE, folded % WIDE + 3
-    twice = (rel + 4 >= WIDE).astype(jnp.int32)
-    scal = jnp.stack(
-        [lon % 2, rel, (lat % 2 == 0).astype(jnp.int32), (lat == lat_count - 1).astype(jnp.int32)]
-    ).astype(jnp.int32)
-    ext_rows = lat * ROWS - HALO + jnp.arange(EXT, dtype=jnp.int32)
-    mirrored = jnp.where(ext_rows >= row_total, 2 * row_total - 1 - ext_rows, ext_rows)
-    spin = coriolis_peak * jnp.sin(math.pi * (mirrored.astype(F32) + 0.5) / row_total - 0.5 * math.pi)
-    valid = ((ext_rows >= 0) & (ext_rows < row_total)).astype(F32)
-    hi, lo = placed_entries(active_index)
-    w1 = jnp.pad(
-        first_weight.reshape(3, 3, CH, INS).transpose(2, 0, 1, 3).reshape(CH, 3, 3 * INS),
-        ((0, 0), (0, 0), (0, TAPK - 3 * INS)),
-    ).reshape(CH, 3 * TAPK)
-    wl = last_weight.reshape(9 * OUTS, CH)
-    wb = last_weight.reshape(3, 3, OUTS, CH)[::-1].reshape(9 * OUTS, CH).T
-    wmt = mix_weight.T
+    entries = active_index.reshape(-1, COLS)
+    first_taps = first_weight.transpose(0, 2, 1)
 
     pla, plb, plc, ce = pl.pallas_call(
         mid_kernel,
         out_shape=(block, block, block, shape((PACK, COLS), BF16)),
         in_specs=[smem()] + vmem(4),
         out_specs=tuple(vmem(4)),
-        compiler_params=params(),
+        compiler_params=params(GRANT),
         name="mid",
-    )(scal, send, bottom, rb, ra)
+    )(scal, send, bottom, ra, rb)
 
     near_a = [(i * lat_count + a, i * lat_count + b) for i in range(lon_count) for a, b in swap_pairs(lat_count, 0)]
     near_b = [
@@ -451,15 +533,16 @@
         return run
 
     branches = [exchange(q, second) for q in range(turns) for second in (False, True)]
-    rlb, rla = lax.switch(2 * turn + twice, branches, pla, plb, plc)
+    rlb, rla = lax.switch(turn.reshape(()), branches, pla, plb, plc)
 
     new_state, closure, active = run_main(
-        scal, spin, valid, own, grad, ce, rla, rlb, w1, mix_weight, wmt, wl, wb, hi, lo
+        row_total, own, grad, ce, rla, rlb, first_taps, mix_weight, last_weight, entries
     )
 
     halves, cores, quads = 2, 2, 4
     inner = lon_count // halves
     everyone = lon_count * lat_count
+    assert inner // cores == lat_count // quads * halves == cores * quads == SHARE
 
     def place_of(d):
         lon_at, lat_at = divmod(d, lat_count)
@@ -470,8 +553,8 @@
         return groups_of(everyone, lambda d: tuple(place_of(d)[i] for i in kept))
 
     total = reduce_over(active, grouped((0, 1, 3)))
-    total = reduce_over(total, grouped((0, 2, 3, 4)))
-    total = reduce_over(total, grouped((1, 2, 4)))
+    total = reduce_over(shared(total), grouped((0, 2, 3, 4)))
+    total = reduce_over(shared(total), grouped((1, 2, 4)))
     return new_state, closure, total.reshape(-1)
 
 

time: 87.2 us -> 85 us (0.975)
  local copies, waits for them, and re-layouts: 6.75 us -> 0.66 us
  blocking collectives: 34.6 us -> 40.6 us
  Pallas kernels: 16.3 us -> 15 us
    all_to_all x3, blocking collectives: 34.6 us -> 40.6 us  [reduce_over(): arrived = lax.all_to_all(shares, BOTH, 0, 0, axis_index_groups=groups)]
    unnamed x17 -> x4, local copies, waits for them, and re-layouts: 5.3 us -> 0.62 us
    pallas_call x1, Pallas kernels: 15.1 us -> 11.4 us  [run_main(): pl.pallas_call(functools.partial(main_kernel, row_total), out_shape=(shap...]
    pallas_call x1, Pallas kernels: 0.62 us -> 1.99 us  [on_device(): pl.pallas_call(functools.partial(prep_kernel, 1.0 / math.sqrt(row_total *...]
    slice x1 -> x0, local copies, waits for them, and re-layouts: 1.2 us -> none  [on_device(): folded = (fold_pair[0] - 3) % col_total]
    pallas_call x1, Pallas kernels: 0.58 us -> 1.56 us  [on_device(): pl.pallas_call(mid_kernel, out_shape=(block, block, block, shape((PACK, C...]
  transfers between devices with their start and end apart: 4 -> 4, of which waited for: 1 -> 2; matrix products, arithmetic and copies ran while one was open for 2% -> 0% of each run, Pallas kernels for 0% -> 0%
where the time goes in v3:
time: 85 us; the launch traced here: 83.3 us
  blocking collectives  40.6 us (48%)
  starting transfers between devices  22.9 us (27%)
  Pallas kernels  15 us (18%)
  waiting for transfers between devices  2.11 us (2%)
  between operations  1.35 us (2%)
    all_to_all x3, blocking collectives, reduce_over(): arrived = lax.all_to_all(shares, BOTH, 0, 0, axis_index_groups=groups)  40.6 us
    ppermute x1, starting transfers between devices, on_device(): ra = lax.ppermute(send, 'lon', swap_pairs(lon_count, 0))  12.1 us
    pallas_call x1, Pallas kernels, run_main(): pl.pallas_call(functools.partial(main_kernel, row_total), out_shape=(shap...  11.4 us
    ppermute x1, starting transfers between devices, run(): return (rlb, lax.ppermute(pla, BOTH, near_a))  4.96 us
    ppermute x1, starting transfers between devices, on_device(): rb = lax.ppermute(send, 'lon', swap_pairs(lon_count, 1))  4.59 us
    pallas_call x1, Pallas kernels, on_device(): pl.pallas_call(functools.partial(prep_kernel, 1.0 / math.sqrt(row_total *...  1.99 us
  transfers between devices with their start and end apart: 4, of which 2 were waited for; matrix products, arithmetic and copies ran while one was open for 0% of the time, Pallas kernels for 0%

profile of v3, /device:TPU:1, one launch (start us, length us, event | category | flops | bytes accessed | tf_op | source)
XLA Modules:
  0.0 83.3 jit_solution(13867957000532158592)
XLA Ops:
  0.6 2.0 %prep.1 = (f32[16,32,128]{2,1,0:T(8,128)}, bf16[16,16,128]{2,1,0:T(8,128)(2,1)}, bf16[5,48,128]{2,1,0:T(8,128)(2,1)}, bf16[4,48,128]{2,1,0:T(8,128)(2,1)}, s32[4]{0:T(128)}, /*index=5*/s32[1]{0:T(128)}) custom-call(f32[3,8,16,128]{3,2,1,0:T(8,128)} %state_hbm.1, f32[8,16,128]{2,1,0:T(8,128)} %kappa_hbm.1, s32[16,128]{1,0:T(8,128)} %depth_hbm.1, ...), custom_call_target="tpu_custom_call" | custom-call | tf_op jit(solution)/shard_map/prep/pallas_call | solution.py:485
  2.6 4.6 %collective-permute-start.81 = (bf16[5,48,128]{2,1,0:T(8,128)(2,1)}, bf16[5,48,128]{2,1,0:T(8,128)(2,1)S(1)}, u32[]{:S(2)}, u32[]{:S(2)}) collective-permute-start(bf16[5,48,128]{2,1,0:T(8,128)(2,1)} %get-tuple-element.261.own_top), channel_id=1, source_target_pairs={{16,32},{32,16},{48,64},{64,48},{80,96},{96,80},{112,128},{128,112... | collective-permute-start | bytes 184328 | tf_op jit(solution)/shard_map/ppermute | solution.py:505
  7.2 12.1 %collective-permute-start.80 = (bf16[5,48,128]{2,1,0:T(8,128)(2,1)}, bf16[5,48,128]{2,1,0:T(8,128)(2,1)S(1)}, u32[]{:S(2)}, u32[]{:S(2)}) collective-permute-start(bf16[5,48,128]{2,1,0:T(8,128)(2,1)} %get-tuple-element.261.own_top), channel_id=1, source_target_pairs={{0,16},{16,0},{32,48},{48,32},{64,80},{80,64},{96,112},{112,96},{1... | collective-permute-start | bytes 184328 | tf_op jit(solution)/shard_map/ppermute | solution.py:506
  20.0 0.0 collective-permute-done.81.rb
  20.0 0.0 copy-start
  20.0 0.4 collective-permute-done.80.ra
  20.4 0.0 copy-start.1
  20.4 0.2 copy-done
  20.6 0.4 copy-done.1
  21.0 1.6 %mid.1 = (bf16[5,48,128]{2,1,0:T(8,128)(2,1)S(1)}, bf16[5,48,128]{2,1,0:T(8,128)(2,1)S(1)}, bf16[5,48,128]{2,1,0:T(8,128)(2,1)S(1)}, bf16[48,128]{1,0:T(8,128)(2,1)}) custom-call(s32[4]{0:T(128)} %get-tuple-element.260.scal, bf16[5,48,128]{2,1,0:T(8,128)(2,1)} %get-tuple-element.261.own_top, bf16[4,48,128]{2,1,0:T(8,128)(2,1)} %get-tuple-element.262.own_bottom, ...), custom_call_target="tpu_custom_call" | custom-call | tf_op jit(solution)/shard_map/mid/pallas_call | solution.py:511
  22.6 7.9 %conditional.1 = (bf16[5,48,128]{2,1,0:T(8,128)(2,1)}, bf16[5,48,128]{2,1,0:T(8,128)(2,1)}) conditional(s32[]{:T(128)} %bitcast, (bf16[5,48,128]{2,1,0:T(8,128)(2,1)S(1)}, bf16[5,48,128]{2,1,0:T(8,128)(2,1)S(1)}) %tuple.136, (bf16[5,48,128]{2,1,0:T(8,128)(2,1)S(1)}, bf16[5,48,128]{2,1,0:T(8,128)(2,1)S(1)}, ...), branch_computations={%region_0.0_spmd, %region_1.0_spmd, %region_2.0_spmd, %region_3.0_... | conditional | flops 30720 | bytes 921736 | solution.py:536
  22.6 1.3 %collective-permute-start.60 = (bf16[5,48,128]{2,1,0:T(8,128)(2,1)S(1)}, bf16[5,48,128]{2,1,0:T(8,128)(2,1)}, u32[]{:S(2)}, u32[]{:S(2)}) collective-permute-start(bf16[5,48,128]{2,1,0:T(8,128)(2,1)S(1)} %get-tuple-element.220), channel_id=1, source_target_pairs={{1,2},{2,1},{3,4},{4,3},{5,6},{6,5},{7,8},{8,7},{9,10},{10,9},{11,... | collective-permute-start | bytes 184328 | tf_op jit(solution)/shard_map/cond/branch_24_fun/ppermute | solution.py:528
  23.9 5.0 %collective-permute-start.61 = (bf16[5,48,128]{2,1,0:T(8,128)(2,1)S(1)}, bf16[5,48,128]{2,1,0:T(8,128)(2,1)}, u32[]{:S(2)}, u32[]{:S(2)}) collective-permute-start(bf16[5,48,128]{2,1,0:T(8,128)(2,1)S(1)} %get-tuple-element.221), channel_id=1, source_target_pairs={{0,1},{1,0},{2,3},{3,2},{4,5},{5,4},{6,7},{7,6},{8,9},{9,8},{10,11... | collective-permute-start | bytes 184328 | tf_op jit(solution)/shard_map/cond/branch_24_fun/ppermute | solution.py:531
  28.8 0.0 collective-permute-done.60
  28.8 1.7 %collective-permute-done.61 = bf16[5,48,128]{2,1,0:T(8,128)(2,1)} collective-permute-done((bf16[5,48,128]{2,1,0:T(8,128)(2,1)S(1)}, bf16[5,48,128]{2,1,0:T(8,128)(2,1)}, u32[]{:S(2)}, u32[]{:S(2)}) %collective-permute-start.61) | collective-permute-done | bytes 61472 | tf_op jit(solution)/shard_map/cond/branch_24_fun/ppermute | solution.py:531
  30.5 11.4 %main.1 = (f32[3,8,16,128]{3,2,1,0:T(8,128)}, bf16[16,16,128]{2,1,0:T(8,128)(2,1)}, bf16[8,64,128]{2,1,0:T(8,128)(2,1)}) custom-call(f32[16,32,128]{2,1,0:T(8,128)} %get-tuple-element.258.own, bf16[16,16,128]{2,1,0:T(8,128)(2,1)} %get-tuple-element.259.grad, bf16[48,128]{1,0:T(8,128)(2,1)} %get-tuple-element.263.ce, ...), custom_call_target="tpu_custom_call" | custom-call | tf_op jit(solution)/shard_map/main/pallas_call | solution.py:438
  42.0 11.1 %all_to_all.15 = bf16[8,64,128]{2,1,0:T(8,128)(2,1)S(1)} all-to-all(bf16[8,64,128]{2,1,0:T(8,128)(2,1)} %get-tuple-element.272), channel_id=1, replica_groups={{0,1,2,3,16,17,18,19},{4,5,6,7,20,21,22,23},{8,9,10,11,24,25,26,27},{12..., dimensions={0} | all-to-all | bytes 262144 | tf_op jit(solution)/shard_map/all_to_all | solution.py:427
  53.2 10.8 %all_to_all.16 = bf16[8,64,128]{2,1,0:T(8,128)(2,1)S(1)} all-to-all(bf16[8,64,128]{2,1,0:T(8,128)(2,1)S(1)} %broadcast_in_dim.4), channel_id=1, replica_groups={{0,32,64,96,128,160,192,224},{1,33,65,97,129,161,193,225},{2,34,66,98,1..., dimensions={0} | all-to-all | bytes 262144 | tf_op jit(solution)/shard_map/all_to_all | solution.py:427
  64.0 18.7 %all_to_all.17 = bf16[8,64,128]{2,1,0:T(8,128)(2,1)S(1)} all-to-all(bf16[8,64,128]{2,1,0:T(8,128)(2,1)S(1)} %broadcast_in_dim.5), channel_id=1, replica_groups={{0,4,8,12,256,260,264,268},{1,5,9,13,257,261,265,269},{2,6,10,14,258,26..., dimensions={0} | all-to-all | bytes 262144 | tf_op jit(solution)/shard_map/all_to_all | solution.py:427
  82.7 0.6 convert_reduce_fusion
  (4 shorter events, 0.1 us)
Async XLA Ops:
  2.6 17.3 %collective-permute-start.81 = (bf16[5,48,128]{2,1,0:T(8,128)(2,1)}, bf16[5,48,128]{2,1,0:T(8,128)(2,1)S(1)}, u32[]{:S(2)}, u32[]{:S(2)}) collective-permute-start(bf16[5,48,128]{2,1,0:T(8,128)(2,1)} %get-tuple-element.261.own_top), channel_id=1, source_target_pairs={{16,32},{32,16},{48,64},{64,48},{80,96},{96,80},{112,128},{128,112... | collective-permute-start | bytes 184328 | tf_op jit(solution)/shard_map/ppermute | solution.py:505
  7.2 13.2 %collective-permute-start.80 = (bf16[5,48,128]{2,1,0:T(8,128)(2,1)}, bf16[5,48,128]{2,1,0:T(8,128)(2,1)S(1)}, u32[]{:S(2)}, u32[]{:S(2)}) collective-permute-start(bf16[5,48,128]{2,1,0:T(8,128)(2,1)} %get-tuple-element.261.own_top), channel_id=1, source_target_pairs={{0,16},{16,0},{32,48},{48,32},{64,80},{80,64},{96,112},{112,96},{1... | collective-permute-start | bytes 184328 | tf_op jit(solution)/shard_map/ppermute | solution.py:506
  20.0 0.6 copy-start
  20.4 0.6 copy-start.1
  22.6 6.2 %collective-permute-start.60 = (bf16[5,48,128]{2,1,0:T(8,128)(2,1)S(1)}, bf16[5,48,128]{2,1,0:T(8,128)(2,1)}, u32[]{:S(2)}, u32[]{:S(2)}) collective-permute-start(bf16[5,48,128]{2,1,0:T(8,128)(2,1)S(1)} %get-tuple-element.220), channel_id=1, source_target_pairs={{1,2},{2,1},{3,4},{4,3},{5,6},{6,5},{7,8},{8,7},{9,10},{10,9},{11,... | collective-permute-start | bytes 184328 | tf_op jit(solution)/shard_map/cond/branch_24_fun/ppermute | solution.py:528
  23.9 6.7 %collective-permute-start.61 = (bf16[5,48,128]{2,1,0:T(8,128)(2,1)S(1)}, bf16[5,48,128]{2,1,0:T(8,128)(2,1)}, u32[]{:S(2)}, u32[]{:S(2)}) collective-permute-start(bf16[5,48,128]{2,1,0:T(8,128)(2,1)S(1)} %get-tuple-element.221), channel_id=1, source_target_pairs={{0,1},{1,0},{2,3},{3,2},{4,5},{5,4},{6,7},{7,6},{8,9},{9,8},{10,11... | collective-permute-start | bytes 184328 | tf_op jit(solution)/shard_map/cond/branch_24_fun/ppermute | solution.py:531
